TPU v7x, 32 devices: a whole 2x2x4 slice. The times are simulated.
32 devices in a mesh: dp: 8 (over z, y), pipe: 4 (over x, core).
Axes of the slice: x: 2, y: 2, z: 4, core: 2. Of those that a mesh axis runs over, the one named last changes fastest.
Arguments:
- inputs: bfloat16 [32, 128, 768], P('dp', 'pipe'), may hold values from -6 to 6
- out_cotangent: bfloat16 [32, 128, 768], P('dp', 'pipe'), may hold values from -6 to 6
- positions: int32 [32, 128], P('dp'), may hold values from 0 to 381, as said below
- norm_gain: bfloat16 [8, 2, 768], P('pipe', None, 'dp'), may hold values from 0.25 to 1.75
- norm_bias: bfloat16 [8, 2, 768], P('pipe', None, 'dp'), may hold values from -1.796875 to 1.796875
- row_bias: bfloat16 [8, 3, 768], P('pipe', None, 'dp'), may hold values from -1.796875 to 1.796875
- w_query: bfloat16 [8, 768, 768], P('pipe', 'dp'), may hold values from -0.21875 to 0.21875
- w_keyval: bfloat16 [4, 768, 128], P('pipe', 'dp'), may hold values from -0.21875 to 0.21875
- keyval_bias: bfloat16 [4, 128], P('pipe', 'dp'), may hold values from -1.796875 to 1.796875
- w_output: bfloat16 [8, 768, 768], P('pipe', 'dp'), may hold values from -1.25 to 1.25
- w_up: bfloat16 [8, 768, 3072], P('pipe', 'dp'), may hold values from -0.21875 to 0.21875
- up_bias: bfloat16 [8, 3072], P('pipe', 'dp'), may hold values from -1.796875 to 1.796875
- w_down: bfloat16 [8, 3072, 768], P('pipe', 'dp'), may hold values from -0.109375 to 0.109375
Outputs:
- final: bfloat16 [32, 128, 768], P('dp', 'pipe')
- input_grad: bfloat16 [32, 128, 768], P('dp', 'pipe')
- grad_norm_gain: float32 [8, 2, 768], P('pipe', None, 'dp')
- grad_norm_bias: float32 [8, 2, 768], P('pipe', None, 'dp')
- grad_row_bias: float32 [8, 3, 768], P('pipe', None, 'dp')
- grad_query: float32 [8, 768, 768], P('pipe', 'dp')
- grad_keyval: float32 [4, 768, 128], P('pipe', 'dp')
- grad_keyval_bias: float32 [4, 128], P('pipe', 'dp')
- grad_output: float32 [8, 768, 768], P('pipe', 'dp')
- grad_up: float32 [8, 768, 3072], P('pipe', 'dp')
- grad_up_bias: float32 [8, 3072], P('pipe', 'dp')
- grad_down: float32 [8, 3072, 768], P('pipe', 'dp')
Inputs may be any that keep to these rules, and one draw needn't show every extreme that they name: Each sequence's positions start at 0 and rise by 1 to 3 from one token to the next; in one sequence they rise by 3 at every step.
All inputs are finite; a program needn't handle non-finite values.
Results may differ from a plain program's by a relative error of at most 0.024.
Values may be sent and summed in bfloat16 or wider, within the bound.
No kernel may reach another device: no remote copies, remote signals or barrier semaphores. Data moves between devices by JAX's collectives and lax.ppermute only.
A program may use at most 256 MiB of HBM per device.

v0:
```python
import math

import jax
import jax.numpy as jnp
from jax import lax
from jax.sharding import PartitionSpec as P

D = 768
HEADS = 12
HEAD_DIM = 64
ROT_DIM = 16


EPSILON = 1e-05
ROPE_BASE = 10000.0
POSITION_SCALE = 4.0
NEG_FILL = -1e30


def from_behind(value, axis, steps):
    count = lax.axis_size(axis)
    leading, last = (max(0, -steps), min(count, count - steps))
    return lax.ppermute(value, axis, [(source, source + steps) for source in range(leading, last)])


def layer_norm(values, norm_gain, norm_shift):
    average = jnp.mean(values, axis=-1, keepdims=True)
    centered = values - average
    variance = jnp.mean(centered * centered, axis=-1, keepdims=True)
    return centered * lax.rsqrt(variance + EPSILON) * norm_gain + norm_shift


def rope_tables(positions):
    half_width = ROT_DIM // 2
    inverse = ROPE_BASE ** (-2.0 * jnp.arange(half_width, dtype=jnp.float32) / ROT_DIM)
    angles = (positions.astype(jnp.float32) / POSITION_SCALE)[..., None] * inverse
    return (jnp.cos(angles), jnp.sin(angles))


def rotate(values, cosine, sine_part):
    half_width = ROT_DIM // 2
    first_half = values[..., :half_width]
    second = values[..., half_width:ROT_DIM]
    return jnp.concatenate(
        [
            first_half * cosine - second * sine_part,
            second * cosine + first_half * sine_part,
            values[..., ROT_DIM:],
        ],
        axis=-1,
    )


def unrotate(grads, cosine, sine_part):
    half_width = ROT_DIM // 2
    first_half = grads[..., :half_width]
    second = grads[..., half_width:ROT_DIM]
    return jnp.concatenate(
        [
            first_half * cosine + second * sine_part,
            second * cosine - first_half * sine_part,
            grads[..., ROT_DIM:],
        ],
        axis=-1,
    )


def gelu_exact(values):
    return jax.nn.gelu(values, approximate=False)


def causal_mask(row_count):
    return lax.broadcasted_iota(jnp.int32, (row_count, row_count), 0) >= lax.broadcasted_iota(
        jnp.int32, (row_count, row_count), 1
    )


def attend(q_rot, key_rot, value_low):
    row_count = q_rot.shape[0]
    grouped = q_rot.reshape(row_count, HEADS, HEAD_DIM)
    scores = jnp.einsum("shd,td->hst", grouped, key_rot, preferred_element_type=jnp.float32) * (
        1.0 / math.sqrt(HEAD_DIM)
    )
    masked = jnp.where(causal_mask(row_count), scores, NEG_FILL)
    row_peak = jnp.max(masked, axis=-1, keepdims=True)
    log_total = row_peak + jnp.log(jnp.sum(jnp.exp(masked - row_peak), axis=-1, keepdims=True))
    probs = jnp.exp(masked - log_total)
    mixed = jnp.einsum(
        "hst,td->shd", probs.astype(jnp.bfloat16), value_low, preferred_element_type=jnp.float32
    )
    return (mixed.reshape(row_count, D).astype(jnp.bfloat16), log_total)


def layer_forward(residual, sublayer, params, cosine, sine_part, shared):
    (
        norm_gain,
        norm_bias,
        row_bias,
        w_query,
        w_keyval,
        keyval_bias,
        w_output,
        w_up,
        up_bias,
        w_down,
    ) = params
    gain_pair = norm_gain[sublayer].astype(jnp.float32)
    shift_pair = norm_bias[sublayer].astype(jnp.float32)
    bias_rows = row_bias[sublayer].astype(jnp.float32)
    row_count = residual.shape[0]
    attn_in = layer_norm(residual, gain_pair[0], shift_pair[0]).astype(jnp.bfloat16)
    mlp_in = layer_norm(residual, gain_pair[1], shift_pair[1]).astype(jnp.bfloat16)
    q_lin = jnp.dot(attn_in, w_query[sublayer], preferred_element_type=jnp.float32) + bias_rows[0]
    q_rot = rotate(
        q_lin.reshape(row_count, HEADS, HEAD_DIM), cosine[:, None, :], sine_part[:, None, :]
    )
    q_rot = q_rot.reshape(row_count, D).astype(jnp.bfloat16)
    if shared is None:
        kv_lin = jnp.dot(attn_in, w_keyval[0], preferred_element_type=jnp.float32) + keyval_bias[
            0
        ].astype(jnp.float32)
        key_rot = rotate(kv_lin[:, :HEAD_DIM], cosine, sine_part).astype(jnp.bfloat16)
        value_low = kv_lin[:, HEAD_DIM:].astype(jnp.bfloat16)
        shared = (key_rot, value_low)
    mixed_low, log_total = attend(q_rot, shared[0], shared[1])
    branch = (
        jnp.dot(mixed_low, w_output[sublayer], preferred_element_type=jnp.float32) + bias_rows[1]
    )
    pre_act = jnp.dot(mlp_in, w_up[sublayer], preferred_element_type=jnp.float32) + up_bias[
        sublayer
    ].astype(jnp.float32)
    act_low = gelu_exact(pre_act).astype(jnp.bfloat16)
    feed_out = jnp.dot(act_low, w_down[sublayer], preferred_element_type=jnp.float32) + bias_rows[2]
    result = residual + branch + feed_out
    return (
        result,
        (residual, attn_in, mlp_in, q_rot, log_total, mixed_low, pre_act, act_low),
        shared,
    )


def section_forward(entering, params, cosine, sine_part):
    residual = entering.astype(jnp.float32)
    residual, kept_first, shared = layer_forward(residual, 0, params, cosine, sine_part, None)
    residual, kept_second, shared = layer_forward(residual, 1, params, cosine, sine_part, shared)
    return (residual.astype(jnp.bfloat16), (kept_first, kept_second, shared[0], shared[1]))


def attention_back(d_mixed, q_rot, key_rot, value_low, log_total):
    row_count = q_rot.shape[0]
    scale = 1.0 / math.sqrt(HEAD_DIM)
    grouped = q_rot.reshape(row_count, HEADS, HEAD_DIM)
    d_grouped = d_mixed.reshape(row_count, HEADS, HEAD_DIM)
    scores = jnp.einsum("shd,td->hst", grouped, key_rot, preferred_element_type=jnp.float32) * scale
    probs = jnp.exp(jnp.where(causal_mask(row_count), scores, NEG_FILL) - log_total)
    d_value = jnp.einsum(
        "hst,shd->td", probs.astype(jnp.bfloat16), d_grouped, preferred_element_type=jnp.float32
    )
    d_probs = jnp.einsum("shd,td->hst", d_grouped, value_low, preferred_element_type=jnp.float32)
    row_dot = jnp.sum(d_probs * probs, axis=-1, keepdims=True)
    d_scores = (probs * (d_probs - row_dot)).astype(jnp.bfloat16)
    d_query = (
        jnp.einsum("hst,td->shd", d_scores, key_rot, preferred_element_type=jnp.float32) * scale
    )
    d_key = jnp.einsum("hst,shd->td", d_scores, grouped, preferred_element_type=jnp.float32) * scale
    return (d_query, d_key, d_value)


def layer_back(d_result, kept_vals, sublayer, params, cosine, sine_part, key_rot, value_low):
    residual, attn_in, mlp_in, q_rot, log_total, mixed_low, pre_act, act_low = kept_vals
    (
        norm_gain,
        norm_bias,
        row_bias,
        w_query,
        w_keyval,
        keyval_bias,
        w_output,
        w_up,
        up_bias,
        w_down,
    ) = params
    row_count = residual.shape[0]
    d_low = d_result.astype(jnp.bfloat16)
    row_grad = jnp.sum(d_low.astype(jnp.float32), axis=0)
    grad_down = jnp.dot(act_low.T, d_low, preferred_element_type=jnp.float32)
    d_act = jnp.dot(d_low, w_down[sublayer].T, preferred_element_type=jnp.float32)
    unused, gelu_pull = jax.vjp(gelu_exact, pre_act)
    d_pre = gelu_pull(d_act)[0].astype(jnp.bfloat16)
    grad_up = jnp.dot(mlp_in.T, d_pre, preferred_element_type=jnp.float32)
    grad_up_bias = jnp.sum(d_pre.astype(jnp.float32), axis=0)
    d_mlp_in = jnp.dot(d_pre, w_up[sublayer].T, preferred_element_type=jnp.float32)
    grad_output = jnp.dot(mixed_low.T, d_low, preferred_element_type=jnp.float32)
    d_mixed = jnp.dot(d_low, w_output[sublayer].T, preferred_element_type=jnp.float32).astype(
        jnp.bfloat16
    )
    d_query, d_key, d_value = attention_back(d_mixed, q_rot, key_rot, value_low, log_total)
    d_qlin = (
        unrotate(d_query, cosine[:, None, :], sine_part[:, None, :])
        .reshape(row_count, D)
        .astype(jnp.bfloat16)
    )
    grad_query = jnp.dot(attn_in.T, d_qlin, preferred_element_type=jnp.float32)
    grad_qbias = jnp.sum(d_qlin.astype(jnp.float32), axis=0)
    d_attn_in = jnp.dot(d_qlin, w_query[sublayer].T, preferred_element_type=jnp.float32)
    bias_grads = jnp.stack([grad_qbias, row_grad, row_grad])
    return (
        d_attn_in,
        d_mlp_in,
        d_key,
        d_value,
        (bias_grads, grad_query, grad_output, grad_up, grad_up_bias, grad_down),
    )


def norm_back(residual, gain_pair, shift_pair, d_attn_in, d_mlp_in):

    def both_norms(values, gain_vals, shift_vals):
        return (
            layer_norm(values, gain_vals[0], shift_vals[0]),
            layer_norm(values, gain_vals[1], shift_vals[1]),
        )

    unused, norm_pull = jax.vjp(both_norms, residual, gain_pair, shift_pair)
    return norm_pull((d_attn_in, d_mlp_in))


def section_back(d_top, kept_all, params, cosine, sine_part):
    kept_first, kept_second, key_rot, value_low = kept_all
    (
        norm_gain,
        norm_bias,
        row_bias,
        w_query,
        w_keyval,
        keyval_bias,
        w_output,
        w_up,
        up_bias,
        w_down,
    ) = params
    attn_one, mlp_one, key_one, value_one, grads_one = layer_back(
        d_top, kept_second, 1, params, cosine, sine_part, key_rot, value_low
    )
    res_one, gain_one, shift_one = norm_back(
        kept_second[0],
        norm_gain[1].astype(jnp.float32),
        norm_bias[1].astype(jnp.float32),
        attn_one,
        mlp_one,
    )
    d_middle = d_top + res_one
    attn_zero, mlp_zero, key_zero, value_zero, grads_zero = layer_back(
        d_middle, kept_first, 0, params, cosine, sine_part, key_rot, value_low
    )
    d_key = unrotate(key_zero + key_one, cosine, sine_part)
    d_keyval = jnp.concatenate([d_key, value_zero + value_one], axis=1).astype(jnp.bfloat16)
    grad_keyval = jnp.dot(kept_first[1].T, d_keyval, preferred_element_type=jnp.float32)
    grad_kv_bias = jnp.sum(d_keyval.astype(jnp.float32), axis=0)
    attn_zero = attn_zero + jnp.dot(d_keyval, w_keyval[0].T, preferred_element_type=jnp.float32)
    res_zero, gain_zero, shift_zero = norm_back(
        kept_first[0],
        norm_gain[0].astype(jnp.float32),
        norm_bias[0].astype(jnp.float32),
        attn_zero,
        mlp_zero,
    )
    d_bottom = d_middle + res_zero
    grads = (
        jnp.stack([gain_zero, gain_one]),
        jnp.stack([shift_zero, shift_one]),
        jnp.stack([grads_zero[0], grads_one[0]]),
        jnp.stack([grads_zero[1], grads_one[1]]),
        grad_keyval[None],
        grad_kv_bias[None],
        jnp.stack([grads_zero[2], grads_one[2]]),
        jnp.stack([grads_zero[3], grads_one[3]]),
        jnp.stack([grads_zero[4], grads_one[4]]),
        jnp.stack([grads_zero[5], grads_one[5]]),
    )
    return (d_bottom.astype(jnp.bfloat16), grads)


def add_trees(left_tree, right_tree):
    return jax.tree.map(lambda left_val, right_val: left_val + right_val, left_tree, right_tree)


def body(
    inputs,
    out_cotangent,
    positions,
    norm_gain,
    norm_bias,
    row_bias,
    w_query,
    w_keyval,
    keyval_bias,
    w_output,
    w_up,
    up_bias,
    w_down,
):
    section_count = lax.axis_size("pipe")
    section_index = lax.axis_index("pipe")
    micro_count = inputs.shape[0]
    step_count = micro_count + section_count - 1
    shards = (
        norm_gain,
        norm_bias,
        row_bias,
        w_query,
        w_keyval,
        keyval_bias,
        w_output,
        w_up,
        up_bias,
        w_down,
    )
    params = (
        lax.all_gather(shards[0], "dp", axis=2, tiled=True),
        lax.all_gather(shards[1], "dp", axis=2, tiled=True),
        lax.all_gather(shards[2], "dp", axis=2, tiled=True),
        lax.all_gather(shards[3], "dp", axis=1, tiled=True),
        lax.all_gather(shards[4], "dp", axis=1, tiled=True),
        lax.all_gather(shards[5], "dp", axis=1, tiled=True),
        lax.all_gather(shards[6], "dp", axis=1, tiled=True),
        lax.all_gather(shards[7], "dp", axis=1, tiled=True),
        lax.all_gather(shards[8], "dp", axis=1, tiled=True),
        lax.all_gather(shards[9], "dp", axis=1, tiled=True),
    )
    whole_in, whole_cot = (
        lax.all_gather(inputs, "pipe", axis=1, tiled=True),
        lax.all_gather(out_cotangent, "pipe", axis=1, tiled=True),
    )
    row_count = whole_in.shape[1]
    cosine_all, sine_all = rope_tables(positions)
    blank = jnp.zeros((row_count, D), jnp.bfloat16)
    stash_init = jnp.zeros_like(whole_in)

    def forward_tick(tick, carried):
        incoming, stash, finals = carried
        micro_index = tick - section_index
        active = (micro_index >= 0) & (micro_index < micro_count)
        slot_index = jnp.clip(micro_index, 0, micro_count - 1)
        fresh = lax.dynamic_index_in_dim(whole_in, slot_index, 0, keepdims=False)
        entering = jnp.where(section_index == 0, fresh, incoming)
        cosine = lax.dynamic_index_in_dim(cosine_all, slot_index, 0, keepdims=False)
        sine_part = lax.dynamic_index_in_dim(sine_all, slot_index, 0, keepdims=False)

        def forward_work(stored):
            leaving, kept_all = section_forward(entering, params, cosine, sine_part)
            stored = lax.dynamic_update_index_in_dim(stored, entering, slot_index, 0)
            return (leaving, stored)

        def forward_resting(stored):
            return (blank, stored)

        leaving, stash = lax.cond(active, forward_work, forward_resting, stash)
        is_last = active & (section_index == section_count - 1)
        finals = jnp.where(
            is_last, lax.dynamic_update_index_in_dim(finals, leaving, slot_index, 0), finals
        )
        incoming = from_behind(leaving, "pipe", 1)
        return (incoming, stash, finals)

    unused_in, stash, finals = lax.fori_loop(
        0, step_count, forward_tick, (blank, stash_init, jnp.zeros_like(whole_in))
    )
    full_zeros = jax.tree.map(lambda weight_arr: jnp.zeros(weight_arr.shape, jnp.float32), params)

    def backward_tick(tick, carried):
        incoming, sums, start_grads = carried
        micro_index = tick - (section_count - 1 - section_index)
        active = (micro_index >= 0) & (micro_index < micro_count)
        slot_index = jnp.clip(micro_index, 0, micro_count - 1)
        given = lax.dynamic_index_in_dim(whole_cot, slot_index, 0, keepdims=False)
        d_top = jnp.where(section_index == section_count - 1, given, incoming).astype(jnp.float32)
        cosine = lax.dynamic_index_in_dim(cosine_all, slot_index, 0, keepdims=False)
        sine_part = lax.dynamic_index_in_dim(sine_all, slot_index, 0, keepdims=False)

        def backward_work(totals):
            entering = lax.dynamic_index_in_dim(stash, slot_index, 0, keepdims=False)
            unused_out, kept_all = section_forward(entering, params, cosine, sine_part)
            d_bottom, grads = section_back(d_top, kept_all, params, cosine, sine_part)
            return (d_bottom, add_trees(totals, grads))

        def backward_resting(totals):
            return (blank, totals)

        d_bottom, sums = lax.cond(active, backward_work, backward_resting, sums)
        is_first = active & (section_index == 0)
        start_grads = jnp.where(
            is_first,
            lax.dynamic_update_index_in_dim(start_grads, d_bottom, slot_index, 0),
            start_grads,
        )
        incoming = from_behind(d_bottom, "pipe", -1)
        return (incoming, sums, start_grads)

    unused_back, sums, start_grads = lax.fori_loop(
        0, step_count, backward_tick, (blank, full_zeros, jnp.zeros_like(whole_in))
    )
    shares = (
        lax.psum_scatter(
            sums[0].astype(jnp.bfloat16), "dp", scatter_dimension=2, tiled=True
        ).astype(jnp.float32),
        lax.psum_scatter(
            sums[1].astype(jnp.bfloat16), "dp", scatter_dimension=2, tiled=True
        ).astype(jnp.float32),
        lax.psum_scatter(
            sums[2].astype(jnp.bfloat16), "dp", scatter_dimension=2, tiled=True
        ).astype(jnp.float32),
        lax.psum_scatter(
            sums[3].astype(jnp.bfloat16), "dp", scatter_dimension=1, tiled=True
        ).astype(jnp.float32),
        lax.psum_scatter(
            sums[4].astype(jnp.bfloat16), "dp", scatter_dimension=1, tiled=True
        ).astype(jnp.float32),
        lax.psum_scatter(
            sums[5].astype(jnp.bfloat16), "dp", scatter_dimension=1, tiled=True
        ).astype(jnp.float32),
        lax.psum_scatter(
            sums[6].astype(jnp.bfloat16), "dp", scatter_dimension=1, tiled=True
        ).astype(jnp.float32),
        lax.psum_scatter(
            sums[7].astype(jnp.bfloat16), "dp", scatter_dimension=1, tiled=True
        ).astype(jnp.float32),
        lax.psum_scatter(
            sums[8].astype(jnp.bfloat16), "dp", scatter_dimension=1, tiled=True
        ).astype(jnp.float32),
        lax.psum_scatter(
            sums[9].astype(jnp.bfloat16), "dp", scatter_dimension=1, tiled=True
        ).astype(jnp.float32),
    )
    out_part = jnp.where(section_index == section_count - 1, finals.astype(jnp.float32), 0.0)
    grad_part = jnp.where(section_index == 0, start_grads.astype(jnp.float32), 0.0)
    final_rows, input_rows = (
        lax.psum_scatter(
            out_part.astype(jnp.bfloat16), "pipe", scatter_dimension=1, tiled=True
        ).astype(jnp.float32),
        lax.psum_scatter(
            grad_part.astype(jnp.bfloat16), "pipe", scatter_dimension=1, tiled=True
        ).astype(jnp.float32),
    )
    return (
        final_rows.astype(jnp.bfloat16),
        input_rows.astype(jnp.bfloat16),
        shares[0],
        shares[1],
        shares[2],
        shares[3],
        shares[4],
        shares[5],
        shares[6],
        shares[7],
        shares[8],
        shares[9],
    )


def solution(mesh):
    return jax.shard_map(
        body,
        mesh=mesh,
        in_specs=(
            P("dp", "pipe", None),
            P("dp", "pipe", None),
            P("dp", None),
            P("pipe", None, "dp"),
            P("pipe", None, "dp"),
            P("pipe", None, "dp"),
            P("pipe", "dp", None),
            P("pipe", "dp", None),
            P("pipe", "dp"),
            P("pipe", "dp", None),
            P("pipe", "dp", None),
            P("pipe", "dp"),
            P("pipe", "dp", None),
        ),
        out_specs=(
            P("dp", "pipe", None),
            P("dp", "pipe", None),
            P("pipe", None, "dp"),
            P("pipe", None, "dp"),
            P("pipe", None, "dp"),
            P("pipe", "dp", None),
            P("pipe", "dp", None),
            P("pipe", "dp"),
            P("pipe", "dp", None),
            P("pipe", "dp", None),
            P("pipe", "dp"),
            P("pipe", "dp", None),
        ),
        check_vma=False,
    )
```

profile of v0, /device:TPU:0, one launch (start us, length us, event | category | flops | bytes accessed | tf_op | source)
XLA Modules:
  0.0 2552.3 jit_solution(37009804579030163)
XLA Ops:
  10.3 33.2 %all_gather.37 = bf16[2,2,768]{1,0,2:T(2,128)(2,1)S(1)} all-gather(bf16[2,2,96]{1,0,2:T(2,128)(2,1)S(1)} %copy.83), channel_id=1, replica_groups=mesh['dp'=8,'pipe'=4] {'dp'}, dimensions={2}, use_global_device_ids=true | all-gather | bytes 6912 | tf_op jit(solution)/shard_map/all_gather | solution.py:320
  44.6 31.8 %all_gather.38 = bf16[2,2,768]{1,0,2:T(2,128)(2,1)S(1)} all-gather(bf16[2,2,96]{1,0,2:T(2,128)(2,1)S(1)} %copy.84), channel_id=1, replica_groups=mesh['dp'=8,'pipe'=4] {'dp'}, dimensions={2}, use_global_device_ids=true | all-gather | bytes 6912 | tf_op jit(solution)/shard_map/all_gather | solution.py:321
  77.4 31.8 %all_gather.42 = bf16[2,3,768]{1,0,2:T(2,128)(2,1)S(1)} all-gather(bf16[2,3,96]{1,0,2:T(2,128)(2,1)S(1)} %copy.85), channel_id=1, replica_groups=mesh['dp'=8,'pipe'=4] {'dp'}, dimensions={2}, use_global_device_ids=true | all-gather | bytes 10368 | tf_op jit(solution)/shard_map/all_gather | solution.py:322
  111.6 22.1 all-reduce.8
  133.8 27.2 %all_gather.45 = bf16[2,3072]{1,0:T(2,128)(2,1)} all-gather(bf16[2,384]{1,0:T(2,128)(2,1)S(1)} %copy-done.151), channel_id=1, replica_groups=mesh['dp'=8,'pipe'=4] {'dp'}, dimensions={1}, use_global_device_ids=true | all-gather | bytes 13824 | tf_op jit(solution)/shard_map/all_gather | solution.py:328
  161.0 33.6 %all_gather.39 = bf16[1,768,128]{2,1,0:T(8,128)(2,1)} all-gather(bf16[1,96,128]{2,1,0:T(8,128)(2,1)S(1)} %copy-done.147), channel_id=1, replica_groups=mesh['dp'=8,'pipe'=4] {'dp'}, dimensions={1}, use_global_device_ids=true | all-gather | bytes 221184 | tf_op jit(solution)/shard_map/all_gather | solution.py:324
  195.7 9.1 all_gather.36
  204.8 9.2 all_gather.47
  213.9 53.0 %all-gather.9.cloned.1.call-done = bf16[2,768,3072]{2,1,0:T(8,128)(2,1)} async-done(((bf16[2,96,3072]{2,1,0:T(8,128)(2,1)}), bf16[2,768,3072]{2,1,0:T(8,128)(2,1)}) %all-gather.9.cloned.1.call-update) | async-done | bytes 9437200 | tf_op jit(solution)/shard_map/all_gather | solution.py:327
  267.0 138.4 %all-gather.11.cloned.1.call-done = bf16[2,3072,768]{2,1,0:T(8,128)(2,1)} async-done(((bf16[2,384,768]{2,1,0:T(8,128)(2,1)}), bf16[2,3072,768]{2,1,0:T(8,128)(2,1)}) %all-gather.11.cloned.1.call-update) | async-done | bytes 9437200 | tf_op jit(solution)/shard_map/all_gather | solution.py:329
  406.5 291.2 %while.62 = (s32[]{:T(128)}, bf16[128,768]{1,0:T(8,128)(2,1)S(1)}, bf16[4,128,768]{2,1,0:T(8,128)(2,1)S(1)}, bf16[4,128,768]{2,1,0:T(8,128)(2,1)}, s32[]{:T(128)...) while((s32[]{:T(128)}, bf16[128,768]{1,0:T(8,128)(2,1)S(1)}, ...), condition=%wide.region_11.12_spmd.clone.clone, body=%wide.region_0.11_spmd.clone.clone.sunk | while | flops 3207243776 | bytes 55717644 | solution.py:366
  407.2 40.7 %conditional.8 = (bf16[128,768]{1,0:T(8,128)(2,1)}, bf16[4,128,768]{2,1,0:T(8,128)(2,1)S(1)}, bf16[1,128,768]{2,1,0:T(8,128)(2,1)}) conditional(s32[]{:T(128)} %convert_element_type.762, bf16[4,128,768]{2,1,0:T(8,128)(2,1)S(1)} %get-tuple-element.2394, (pred[]{:T(512)}, bf16[4,128,768]{2,1,0:T(8,128)(2,1)}, s32[]{:T(128)}, ...), branch_computations={%region_1.1_spmd, %region_2.10_spmd} | conditional | flops 3207141376 | bytes 54321956 | solution.py:358
  412.8 8.1 fusion.54
  429.4 8.1 fusion.57
  451.7 40.7 %conditional.8 = (bf16[128,768]{1,0:T(8,128)(2,1)}, bf16[4,128,768]{2,1,0:T(8,128)(2,1)S(1)}, bf16[1,128,768]{2,1,0:T(8,128)(2,1)}) conditional(s32[]{:T(128)} %convert_element_type.762, bf16[4,128,768]{2,1,0:T(8,128)(2,1)S(1)} %get-tuple-element.2394, (pred[]{:T(512)}, bf16[4,128,768]{2,1,0:T(8,128)(2,1)}, s32[]{:T(128)}, ...), branch_computations={%region_1.1_spmd, %region_2.10_spmd} | conditional | flops 3207141376 | bytes 54321956 | solution.py:358
  457.2 8.1 fusion.54
  473.8 8.1 fusion.57
  496.7 40.7 %conditional.8 = (bf16[128,768]{1,0:T(8,128)(2,1)}, bf16[4,128,768]{2,1,0:T(8,128)(2,1)S(1)}, bf16[1,128,768]{2,1,0:T(8,128)(2,1)}) conditional(s32[]{:T(128)} %convert_element_type.762, bf16[4,128,768]{2,1,0:T(8,128)(2,1)S(1)} %get-tuple-element.2394, (pred[]{:T(512)}, bf16[4,128,768]{2,1,0:T(8,128)(2,1)}, s32[]{:T(128)}, ...), branch_computations={%region_1.1_spmd, %region_2.10_spmd} | conditional | flops 3207141376 | bytes 54321956 | solution.py:358
  502.2 8.1 fusion.54
  518.8 8.1 fusion.57
  543.0 40.7 %conditional.8 = (bf16[128,768]{1,0:T(8,128)(2,1)}, bf16[4,128,768]{2,1,0:T(8,128)(2,1)S(1)}, bf16[1,128,768]{2,1,0:T(8,128)(2,1)}) conditional(s32[]{:T(128)} %convert_element_type.762, bf16[4,128,768]{2,1,0:T(8,128)(2,1)S(1)} %get-tuple-element.2394, (pred[]{:T(512)}, bf16[4,128,768]{2,1,0:T(8,128)(2,1)}, s32[]{:T(128)}, ...), branch_computations={%region_1.1_spmd, %region_2.10_spmd} | conditional | flops 3207141376 | bytes 54321956 | solution.py:358
  548.5 8.1 fusion.54
  565.1 8.1 fusion.57
  593.0 44.8 %collective-permute-start = (bf16[128,768]{1,0:T(8,128)(2,1)}, bf16[128,768]{1,0:T(8,128)(2,1)S(1)}, u32[]{:S(2)}, u32[]{:S(2)}) collective-permute-start(bf16[128,768]{1,0:T(8,128)(2,1)} %get-tuple-element.2293), channel_id=1, source_target_pairs={{0,1},{1,2},{2,3},{4,5},{5,6},{6,7},{8,9},{9,10},{10,11},{12,13},{... | collective-permute-start | bytes 589832 | tf_op jit(solution)/shard_map/while/body/eval_jaxpr/ppermute | solution.py:23
  651.0 44.8 %collective-permute-start = (bf16[128,768]{1,0:T(8,128)(2,1)}, bf16[128,768]{1,0:T(8,128)(2,1)S(1)}, u32[]{:S(2)}, u32[]{:S(2)}) collective-permute-start(bf16[128,768]{1,0:T(8,128)(2,1)} %get-tuple-element.2293), channel_id=1, source_target_pairs={{0,1},{1,2},{2,3},{4,5},{5,6},{6,7},{8,9},{9,10},{10,11},{12,13},{... | collective-permute-start | bytes 589832 | tf_op jit(solution)/shard_map/while/body/eval_jaxpr/ppermute | solution.py:23
  702.7 8.9 broadcast_in_dim.233
  712.2 7.7 broadcast_in_dim.235
  720.8 922.9 %while.63 = (s32[]{:T(128)}, bf16[128,768]{1,0:T(8,128)(2,1)S(1)}, f32[2,2,768]{2,1,0:T(2,128)S(1)}, f32[2,2,768]{2,1,0:T(2,128)S(1)}, f32[2,3,768]{2,1,0:T(4,12...) while((s32[]{:T(128)}, bf16[128,768]{1,0:T(8,128)(2,1)S(1)}, ...), condition=%wide.region_49.50_spmd.clone.clone, body=%wide.region_13.49_spmd.clone.clone.sunk | while | flops 8820883456 | bytes 665309568 | solution.py:400
  757.2 36.9 %collective-permute-done.1 = bf16[128,768]{1,0:T(8,128)(2,1)S(1)} collective-permute-done((bf16[128,768]{1,0:T(8,128)(2,1)}, bf16[128,768]{1,0:T(8,128)(2,1)S(1)}, u32[]{:S(2)}, u32[]{:S(2)}) %collective-permute-start.1) | collective-permute-done | bytes 196640 | tf_op jit(solution)/shard_map/while/body/eval_jaxpr/ppermute | solution.py:23
  800.2 345.0 %collective-permute-done.1 = bf16[128,768]{1,0:T(8,128)(2,1)S(1)} collective-permute-done((bf16[128,768]{1,0:T(8,128)(2,1)}, bf16[128,768]{1,0:T(8,128)(2,1)S(1)}, u32[]{:S(2)}, u32[]{:S(2)}) %collective-permute-start.1) | collective-permute-done | bytes 196640 | tf_op jit(solution)/shard_map/while/body/eval_jaxpr/ppermute | solution.py:23
  1146.9 116.6 %conditional.9 = (bf16[128,768]{1,0:T(8,128)(2,1)}, f32[2,2,768]{2,1,0:T(2,128)S(1)}, f32[2,2,768]{2,1,0:T(2,128)S(1)}, f32[2,3,768]{2,1,0:T(4,128)S(1)}, f32[2,...) conditional(s32[]{:T(128)} %convert_element_type.764, ...), branch_computations={%region_14.14_spmd, %region_15.48_spmd} | conditional | flops 8820584448 | bytes 663127296 | solution.py:390
  1151.9 8.3 multiply_convert_fusion.1
  1223.9 17.4 maximum_add_fusion
  1241.4 6.9 convolution_bitcast_fusion
  1249.8 7.1 maximum_add_fusion.1
  1272.4 116.6 %conditional.9 = (bf16[128,768]{1,0:T(8,128)(2,1)}, f32[2,2,768]{2,1,0:T(2,128)S(1)}, f32[2,2,768]{2,1,0:T(2,128)S(1)}, f32[2,3,768]{2,1,0:T(4,128)S(1)}, f32[2,...) conditional(s32[]{:T(128)} %convert_element_type.764, ...), branch_computations={%region_14.14_spmd, %region_15.48_spmd} | conditional | flops 8820584448 | bytes 663127296 | solution.py:390
  1277.4 8.3 multiply_convert_fusion.1
  1349.4 17.4 maximum_add_fusion
  1366.9 6.9 convolution_bitcast_fusion
  1375.3 7.1 maximum_add_fusion.1
  1397.9 116.6 %conditional.9 = (bf16[128,768]{1,0:T(8,128)(2,1)}, f32[2,2,768]{2,1,0:T(2,128)S(1)}, f32[2,2,768]{2,1,0:T(2,128)S(1)}, f32[2,3,768]{2,1,0:T(4,128)S(1)}, f32[2,...) conditional(s32[]{:T(128)} %convert_element_type.764, ...), branch_computations={%region_14.14_spmd, %region_15.48_spmd} | conditional | flops 8820584448 | bytes 663127296 | solution.py:390
  1402.9 8.3 multiply_convert_fusion.1
  1474.9 17.4 maximum_add_fusion
  1492.4 6.9 convolution_bitcast_fusion
  1500.9 7.1 maximum_add_fusion.1
  1523.5 116.6 %conditional.9 = (bf16[128,768]{1,0:T(8,128)(2,1)}, f32[2,2,768]{2,1,0:T(2,128)S(1)}, f32[2,2,768]{2,1,0:T(2,128)S(1)}, f32[2,3,768]{2,1,0:T(4,128)S(1)}, f32[2,...) conditional(s32[]{:T(128)} %convert_element_type.764, ...), branch_computations={%region_14.14_spmd, %region_15.48_spmd} | conditional | flops 8820584448 | bytes 663127296 | solution.py:390
  1528.4 8.3 multiply_convert_fusion.1
  1600.4 17.4 maximum_add_fusion
  1617.9 6.9 convolution_bitcast_fusion
  1626.4 7.1 maximum_add_fusion.1
  1660.1 10.0 convert_element_type.541
  1670.2 11.2 convert_element_type.545
  1684.7 11.0 reduce-scatter.43.cloned.1.call-done
  1697.0 62.6 %reduce-scatter.37.cloned.1.call-done = bf16[96,4]{1,0:T(8,128)(2,1)} async-done(((bf16[768,4]{1,0:T(8,128)(2,1)}), bf16[96,4]{1,0:T(8,128)(2,1)}) %reduce-scatter.37.cloned.1.call-update) | async-done | bytes 784
  1761.0 62.5 %reduce-scatter.39.cloned.1.call-done = bf16[96,4]{1,0:T(8,128)(2,1)} async-done(((bf16[768,4]{1,0:T(8,128)(2,1)}), bf16[96,4]{1,0:T(8,128)(2,1)}) %reduce-scatter.39.cloned.1.call-update) | async-done | bytes 784
  1825.1 61.9 %reduce-scatter.41.cloned.1.call-done = bf16[96,6]{1,0:T(8,128)(2,1)} async-done(((bf16[768,6]{1,0:T(8,128)(2,1)}), bf16[96,6]{1,0:T(8,128)(2,1)}) %reduce-scatter.41.cloned.1.call-update) | async-done | bytes 1168
  1888.5 63.3 %reduce-scatter.45.cloned.1.call-done = bf16[384,2]{1,0:T(8,128)(2,1)} async-done(((bf16[3072,2]{1,0:T(8,128)(2,1)}), bf16[384,2]{1,0:T(8,128)(2,1)}) %reduce-scatter.45.cloned.1.call-update) | async-done | bytes 1552
  1953.4 62.0 %reduce-scatter.29.cloned.1.call-done = bf16[1,96,128]{2,1,0:T(8,128)(2,1)} async-done(((bf16[1,768,128]{2,1,0:T(8,128)(2,1)}), bf16[1,96,128]{2,1,0:T(8,128)(2,1)}) %reduce-scatter.29.cloned.1.call-update) | async-done | bytes 24592 | tf_op jit(solution)/shard_map/reduce_scatter | solution.py:416
  2016.8 71.4 %reduce-scatter.27.cloned.1.call-done = bf16[2,96,768]{2,1,0:T(8,128)(2,1)} async-done(((bf16[2,768,768]{2,1,0:T(8,128)(2,1)}), bf16[2,96,768]{2,1,0:T(8,128)(2,1)}) %reduce-scatter.27.cloned.1.call-update) | async-done | bytes 294928 | tf_op jit(solution)/shard_map/reduce_scatter | solution.py:413
  2090.0 70.8 %reduce-scatter.31.cloned.1.call-done = bf16[2,96,768]{2,1,0:T(8,128)(2,1)} async-done(((bf16[2,768,768]{2,1,0:T(8,128)(2,1)}), bf16[2,96,768]{2,1,0:T(8,128)(2,1)}) %reduce-scatter.31.cloned.1.call-update) | async-done | bytes 294928 | tf_op jit(solution)/shard_map/reduce_scatter | solution.py:422
  2162.6 164.8 %reduce-scatter.33.cloned.1.call-done = bf16[2,96,3072]{2,1,0:T(8,128)(2,1)} async-done(((bf16[2,768,3072]{2,1,0:T(8,128)(2,1)}), bf16[2,96,3072]{2,1,0:T(8,128)(2,1)}) %reduce-scatter.33.cloned.1.call-update) | async-done | bytes 1179664 | tf_op jit(solution)/shard_map/reduce_scatter | solution.py:425
  2330.3 163.4 %reduce-scatter.35.cloned.1.call-done = bf16[2,384,768]{2,1,0:T(8,128)(2,1)} async-done(((bf16[2,3072,768]{2,1,0:T(8,128)(2,1)}), bf16[2,384,768]{2,1,0:T(8,128)(2,1)}) %reduce-scatter.35.cloned.1.call-update) | async-done | bytes 1179664 | tf_op jit(solution)/shard_map/reduce_scatter | solution.py:431
  2496.5 22.7 reduce-scatter.23.cloned.1.call-done
  2519.2 26.2 %reduce-scatter.25.cloned.1.call-done = bf16[4,32,768]{2,1,0:T(8,128)(2,1)} async-done(((bf16[4,128,768]{2,1,0:T(8,128)(2,1)}), bf16[4,32,768]{2,1,0:T(8,128)(2,1)}) %reduce-scatter.25.cloned.1.call-update) | async-done | bytes 196624 | tf_op jit(solution)/shard_map/reduce_scatter | solution.py:441
  (2099 shorter events, 548.7 us)
Async XLA Ops:
  7.2 206.7 %all-gather.5.cloned.1.call-start = ((), (), s32[]{:S(2)}) async-start(), calls=%async_computation.12 | async-start | bytes 2654208 | tf_op jit(solution)/shard_map/all_gather | solution.py:323
  7.9 206.0 %all-gather.7.cloned.1.call-start = ((), (), s32[]{:S(2)}) async-start(), calls=%async_computation.13 | async-start | bytes 2654208 | tf_op jit(solution)/shard_map/all_gather | solution.py:326
  8.7 35.7 %copy-start.153 = (bf16[2,2,96]{2,1,0:T(2,128)(2,1)S(1)}, bf16[2,2,96]{2,1,0:T(2,128)(2,1)}, u32[]{:S(2)}) copy-start(bf16[2,2,96]{2,1,0:T(2,128)(2,1)} %param.25) | copy-start | bytes 2308
  8.7 258.3 %all-gather.9.cloned.1.call-start = ((), (), s32[]{:S(2)}) async-start(), calls=%async_computation.14 | async-start | bytes 10616832 | tf_op jit(solution)/shard_map/all_gather | solution.py:327
  9.4 67.9 %copy-start.150 = (bf16[2,3,96]{2,0,1:T(2,128)(2,1)S(1)}, bf16[2,3,96]{2,0,1:T(2,128)(2,1)}, u32[]{:S(2)}) copy-start(bf16[2,3,96]{2,0,1:T(2,128)(2,1)} %param.26) | copy-start | bytes 3460
  9.4 396.0 %all-gather.11.cloned.1.call-start = ((), (), s32[]{:S(2)}) async-start(), calls=%async_computation.15 | async-start | bytes 10616832 | tf_op jit(solution)/shard_map/all_gather | solution.py:329
  10.0 100.1 %copy-start.157 = (u32[32]{0:T(128)S(1)}, u32[32]{0:T(128)}, u32[]{:S(2)}) copy-start(u32[32]{0:T(128)} %constant.505) | copy-start | bytes 388
  10.0 101.3 %copy-start.156 = (bf16[1,16]{1,0:T(2,128)(2,1)S(1)}, bf16[1,16]{1,0:T(2,128)(2,1)}, u32[]{:S(2)}) copy-start(bf16[1,16]{1,0:T(2,128)(2,1)} %param.29) | copy-start | bytes 100
  10.0 123.7 %copy-start.151 = (bf16[2,384]{1,0:T(2,128)(2,1)S(1)}, bf16[2,384]{1,0:T(2,128)(2,1)}, u32[]{:S(2)}) copy-start(bf16[2,384]{1,0:T(2,128)(2,1)} %param.32) | copy-start | bytes 4612
  10.0 150.9 %copy-start.147 = (bf16[1,96,128]{2,1,0:T(8,128)(2,1)S(1)}, bf16[1,96,128]{2,1,0:T(8,128)(2,1)}, u32[]{:S(2)}) copy-start(bf16[1,96,128]{2,1,0:T(8,128)(2,1)} %param.28) | copy-start | bytes 73732
  10.0 185.0 %copy-start.149 = (s32[4,128]{1,0:T(4,128)S(1)}, s32[4,128]{1,0:T(4,128)}, u32[]{:S(2)}) copy-start(s32[4,128]{1,0:T(4,128)} %param.23) | copy-start | bytes 6148
  10.1 185.6 %copy-start.133 = (bf16[4,32,768]{2,1,0:T(8,128)(2,1)S(1)}, bf16[4,32,768]{2,1,0:T(8,128)(2,1)}, u32[]{:S(2)}) copy-start(bf16[4,32,768]{2,1,0:T(8,128)(2,1)} %param.21) | copy-start | bytes 589828
  10.1 1685.6 %reduce-scatter.43.cloned.1.call-start = ((), (), s32[]{:S(2)}) async-start(), calls=%async_computation.26 | async-start | bytes 36864
  44.4 160.4 %copy-start.134 = (bf16[4,32,768]{2,1,0:T(8,128)(2,1)S(1)}, bf16[4,32,768]{2,1,0:T(8,128)(2,1)}, u32[]{:S(2)}) copy-start(bf16[4,32,768]{2,1,0:T(8,128)(2,1)} %param.22) | copy-start | bytes 589828
  448.0 3.0 collective-permute-start
  492.4 3.5 collective-permute-start
  537.4 4.8 collective-permute-start
  583.7 7.2 collective-permute-start
  593.0 46.5 %collective-permute-start = (bf16[128,768]{1,0:T(8,128)(2,1)}, bf16[128,768]{1,0:T(8,128)(2,1)S(1)}, u32[]{:S(2)}, u32[]{:S(2)}) collective-permute-start(bf16[128,768]{1,0:T(8,128)(2,1)} %get-tuple-element.2293), channel_id=1, source_target_pairs={{0,1},{1,2},{2,3},{4,5},{5,6},{6,7},{8,9},{9,10},{10,11},{12,13},{... | collective-permute-start | bytes 589832 | tf_op jit(solution)/shard_map/while/body/eval_jaxpr/ppermute | solution.py:23
  641.7 7.2 collective-permute-start
  651.0 46.5 %collective-permute-start = (bf16[128,768]{1,0:T(8,128)(2,1)}, bf16[128,768]{1,0:T(8,128)(2,1)S(1)}, u32[]{:S(2)}, u32[]{:S(2)}) collective-permute-start(bf16[128,768]{1,0:T(8,128)(2,1)} %get-tuple-element.2293), channel_id=1, source_target_pairs={{0,1},{1,2},{2,3},{4,5},{5,6},{6,7},{8,9},{9,10},{10,11},{12,13},{... | collective-permute-start | bytes 589832 | tf_op jit(solution)/shard_map/while/body/eval_jaxpr/ppermute | solution.py:23
  744.5 6.7 collective-permute-start.1
  754.2 39.9 %collective-permute-start.1 = (bf16[128,768]{1,0:T(8,128)(2,1)}, bf16[128,768]{1,0:T(8,128)(2,1)S(1)}, u32[]{:S(2)}, u32[]{:S(2)}) collective-permute-start(bf16[128,768]{1,0:T(8,128)(2,1)} %get-tuple-element.2326), channel_id=1, source_target_pairs={{1,0},{2,1},{3,2},{5,4},{6,5},{7,6},{9,8},{10,9},{11,10},{13,12},{... | collective-permute-start | bytes 589832 | tf_op jit(solution)/shard_map/while/body/eval_jaxpr/ppermute | solution.py:23
  797.2 348.0 %collective-permute-start.1 = (bf16[128,768]{1,0:T(8,128)(2,1)}, bf16[128,768]{1,0:T(8,128)(2,1)S(1)}, u32[]{:S(2)}, u32[]{:S(2)}) collective-permute-start(bf16[128,768]{1,0:T(8,128)(2,1)} %get-tuple-element.2326), channel_id=1, source_target_pairs={{1,0},{2,1},{3,2},{5,4},{6,5},{7,6},{9,8},{10,9},{11,10},{13,12},{... | collective-permute-start | bytes 589832 | tf_op jit(solution)/shard_map/while/body/eval_jaxpr/ppermute | solution.py:23
  1165.8 28.8 %copy-start.42 = (f32[128,8]{0,1:T(8,128)}, f32[128,8]{0,1:T(8,128)S(1)}, u32[]{:S(2)}) copy-start(f32[128,8]{0,1:T(8,128)S(1)} %get-tuple-element.1932) | copy-start | bytes 12292 | tf_op jit(solution)/shard_map/while/body/eval_jaxpr/cond
  1165.8 28.8 %copy-start.44 = (f32[128,8]{0,1:T(8,128)}, f32[128,8]{0,1:T(8,128)S(1)}, u32[]{:S(2)}) copy-start(f32[128,8]{0,1:T(8,128)S(1)} %get-tuple-element.1933) | copy-start | bytes 12292 | tf_op jit(solution)/shard_map/while/body/eval_jaxpr/cond
  1223.8 17.5 copy-start.72
  1223.8 17.5 copy-start.163
  1223.8 25.9 %slice-start = ((s8[18874368]{0:T(1024)(128)(4,1)}), s8[2097152]{0:T(1024)(128)(4,1)S(1)}, s32[]{:S(2)}) async-start(s8[18874368]{0:T(1024)(128)(4,1)} %bitcast.396), calls=%async_computation.28 | async-start | bytes 4194304 | tf_op jit(solution)/shard_map/while/body/eval_jaxpr/cond
  1223.9 25.9 %slice-start.1 = ((s8[18874368]{0:T(1024)(128)(4,1)}), s8[4194304]{0:T(1024)(128)(4,1)S(1)}, s32[]{:S(2)}) async-start(s8[18874368]{0:T(1024)(128)(4,1)} %bitcast.396), calls=%async_computation.29 | async-start | bytes 8388608 | tf_op jit(solution)/shard_map/while/body/eval_jaxpr/cond
  1223.9 25.9 %slice-start.2 = ((s8[18874368]{0:T(1024)(128)(4,1)}), s8[4194304]{0:T(1024)(128)(4,1)S(1)}, s32[]{:S(2)}) async-start(s8[18874368]{0:T(1024)(128)(4,1)} %bitcast.396), calls=%async_computation.30 | async-start | bytes 8388608 | tf_op jit(solution)/shard_map/while/body/eval_jaxpr/cond
  1263.5 7.2 collective-permute-start.1
  1291.3 28.8 %copy-start.42 = (f32[128,8]{0,1:T(8,128)}, f32[128,8]{0,1:T(8,128)S(1)}, u32[]{:S(2)}) copy-start(f32[128,8]{0,1:T(8,128)S(1)} %get-tuple-element.1932) | copy-start | bytes 12292 | tf_op jit(solution)/shard_map/while/body/eval_jaxpr/cond
  1291.4 28.8 %copy-start.44 = (f32[128,8]{0,1:T(8,128)}, f32[128,8]{0,1:T(8,128)S(1)}, u32[]{:S(2)}) copy-start(f32[128,8]{0,1:T(8,128)S(1)} %get-tuple-element.1933) | copy-start | bytes 12292 | tf_op jit(solution)/shard_map/while/body/eval_jaxpr/cond
  1349.3 17.5 copy-start.163
  1349.4 25.9 %slice-start = ((s8[18874368]{0:T(1024)(128)(4,1)}), s8[2097152]{0:T(1024)(128)(4,1)S(1)}, s32[]{:S(2)}) async-start(s8[18874368]{0:T(1024)(128)(4,1)} %bitcast.396), calls=%async_computation.28 | async-start | bytes 4194304 | tf_op jit(solution)/shard_map/while/body/eval_jaxpr/cond
  1349.4 25.9 %slice-start.1 = ((s8[18874368]{0:T(1024)(128)(4,1)}), s8[4194304]{0:T(1024)(128)(4,1)S(1)}, s32[]{:S(2)}) async-start(s8[18874368]{0:T(1024)(128)(4,1)} %bitcast.396), calls=%async_computation.29 | async-start | bytes 8388608 | tf_op jit(solution)/shard_map/while/body/eval_jaxpr/cond
  1349.4 25.9 %slice-start.2 = ((s8[18874368]{0:T(1024)(128)(4,1)}), s8[4194304]{0:T(1024)(128)(4,1)S(1)}, s32[]{:S(2)}) async-start(s8[18874368]{0:T(1024)(128)(4,1)} %bitcast.396), calls=%async_computation.30 | async-start | bytes 8388608 | tf_op jit(solution)/shard_map/while/body/eval_jaxpr/cond
  1389.0 7.2 collective-permute-start.1
  1416.8 28.8 %copy-start.42 = (f32[128,8]{0,1:T(8,128)}, f32[128,8]{0,1:T(8,128)S(1)}, u32[]{:S(2)}) copy-start(f32[128,8]{0,1:T(8,128)S(1)} %get-tuple-element.1932) | copy-start | bytes 12292 | tf_op jit(solution)/shard_map/while/body/eval_jaxpr/cond
  1416.9 28.8 %copy-start.44 = (f32[128,8]{0,1:T(8,128)}, f32[128,8]{0,1:T(8,128)S(1)}, u32[]{:S(2)}) copy-start(f32[128,8]{0,1:T(8,128)S(1)} %get-tuple-element.1933) | copy-start | bytes 12292 | tf_op jit(solution)/shard_map/while/body/eval_jaxpr/cond
  1474.9 17.5 copy-start.163
  1474.9 25.9 %slice-start = ((s8[18874368]{0:T(1024)(128)(4,1)}), s8[2097152]{0:T(1024)(128)(4,1)S(1)}, s32[]{:S(2)}) async-start(s8[18874368]{0:T(1024)(128)(4,1)} %bitcast.396), calls=%async_computation.28 | async-start | bytes 4194304 | tf_op jit(solution)/shard_map/while/body/eval_jaxpr/cond
  1474.9 25.9 %slice-start.1 = ((s8[18874368]{0:T(1024)(128)(4,1)}), s8[4194304]{0:T(1024)(128)(4,1)S(1)}, s32[]{:S(2)}) async-start(s8[18874368]{0:T(1024)(128)(4,1)} %bitcast.396), calls=%async_computation.29 | async-start | bytes 8388608 | tf_op jit(solution)/shard_map/while/body/eval_jaxpr/cond
  1474.9 25.9 %slice-start.2 = ((s8[18874368]{0:T(1024)(128)(4,1)}), s8[4194304]{0:T(1024)(128)(4,1)S(1)}, s32[]{:S(2)}) async-start(s8[18874368]{0:T(1024)(128)(4,1)} %bitcast.396), calls=%async_computation.30 | async-start | bytes 8388608 | tf_op jit(solution)/shard_map/while/body/eval_jaxpr/cond
  1514.5 7.2 collective-permute-start.1
  1542.4 28.8 %copy-start.42 = (f32[128,8]{0,1:T(8,128)}, f32[128,8]{0,1:T(8,128)S(1)}, u32[]{:S(2)}) copy-start(f32[128,8]{0,1:T(8,128)S(1)} %get-tuple-element.1932) | copy-start | bytes 12292 | tf_op jit(solution)/shard_map/while/body/eval_jaxpr/cond
  1542.4 28.8 %copy-start.44 = (f32[128,8]{0,1:T(8,128)}, f32[128,8]{0,1:T(8,128)S(1)}, u32[]{:S(2)}) copy-start(f32[128,8]{0,1:T(8,128)S(1)} %get-tuple-element.1933) | copy-start | bytes 12292 | tf_op jit(solution)/shard_map/while/body/eval_jaxpr/cond
  1600.4 17.5 copy-start.163
  1600.4 25.9 %slice-start = ((s8[18874368]{0:T(1024)(128)(4,1)}), s8[2097152]{0:T(1024)(128)(4,1)S(1)}, s32[]{:S(2)}) async-start(s8[18874368]{0:T(1024)(128)(4,1)} %bitcast.396), calls=%async_computation.28 | async-start | bytes 4194304 | tf_op jit(solution)/shard_map/while/body/eval_jaxpr/cond
  1600.4 25.9 %slice-start.1 = ((s8[18874368]{0:T(1024)(128)(4,1)}), s8[4194304]{0:T(1024)(128)(4,1)S(1)}, s32[]{:S(2)}) async-start(s8[18874368]{0:T(1024)(128)(4,1)} %bitcast.396), calls=%async_computation.29 | async-start | bytes 8388608 | tf_op jit(solution)/shard_map/while/body/eval_jaxpr/cond
  1600.4 25.9 %slice-start.2 = ((s8[18874368]{0:T(1024)(128)(4,1)}), s8[4194304]{0:T(1024)(128)(4,1)S(1)}, s32[]{:S(2)}) async-start(s8[18874368]{0:T(1024)(128)(4,1)} %bitcast.396), calls=%async_computation.30 | async-start | bytes 8388608 | tf_op jit(solution)/shard_map/while/body/eval_jaxpr/cond
  1640.0 3.5 collective-permute-start.1
  1644.6 115.0 %reduce-scatter.37.cloned.1.call-start = ((), (), s32[]{:S(2)}) async-start(), calls=%async_computation.23 | async-start | bytes 221184
  1646.0 177.5 %reduce-scatter.39.cloned.1.call-start = ((), (), s32[]{:S(2)}) async-start(), calls=%async_computation.24 | async-start | bytes 221184
  1648.1 238.8 %reduce-scatter.41.cloned.1.call-start = ((), (), s32[]{:S(2)}) async-start(), calls=%async_computation.25 | async-start | bytes 221184
  1649.9 302.0 %reduce-scatter.45.cloned.1.call-start = ((), (), s32[]{:S(2)}) async-start(), calls=%async_computation.27 | async-start | bytes 884736
  1651.2 364.2 %reduce-scatter.29.cloned.1.call-start = ((), (), s32[]{:S(2)}) async-start(), calls=%async_computation.19 | async-start | bytes 221184 | tf_op jit(solution)/shard_map/reduce_scatter | solution.py:416
  1652.0 436.2 %reduce-scatter.27.cloned.1.call-start = ((), (), s32[]{:S(2)}) async-start(), calls=%async_computation.18 | async-start | bytes 2654208 | tf_op jit(solution)/shard_map/reduce_scatter | solution.py:413
  1656.0 504.8 %reduce-scatter.31.cloned.1.call-start = ((), (), s32[]{:S(2)}) async-start(), calls=%async_computation.20 | async-start | bytes 2654208 | tf_op jit(solution)/shard_map/reduce_scatter | solution.py:422
  1660.1 667.3 %reduce-scatter.33.cloned.1.call-start = ((), (), s32[]{:S(2)}) async-start(), calls=%async_computation.21 | async-start | bytes 10616832 | tf_op jit(solution)/shard_map/reduce_scatter | solution.py:425
  1670.2 823.5 %reduce-scatter.35.cloned.1.call-start = ((), (), s32[]{:S(2)}) async-start(), calls=%async_computation.22 | async-start | bytes 10616832 | tf_op jit(solution)/shard_map/reduce_scatter | solution.py:431
  1681.4 837.7 %reduce-scatter.23.cloned.1.call-start = ((), (), s32[]{:S(2)}) async-start(), calls=%async_computation.16 | async-start | bytes 983040 | tf_op jit(solution)/shard_map/reduce_scatter | solution.py:438
  1683.6 861.8 %reduce-scatter.25.cloned.1.call-start = ((), (), s32[]{:S(2)}) async-start(), calls=%async_computation.17 | async-start | bytes 983040 | tf_op jit(solution)/shard_map/reduce_scatter | solution.py:441
  (614 other events, 2353.2 us)
Sparse Core Ops, SparseCore 0:
  10.2 61.5 all-gather.4
  74.0 52.1 all-gather.6
  128.3 138.6 all-gather.8
  269.0 136.3 all-gather.10
  1644.7 50.9 reduce-scatter.42
  1699.4 60.1 reduce-scatter.36
  1763.4 60.1 reduce-scatter.38
  1826.8 60.1 reduce-scatter.40
  1890.3 61.5 reduce-scatter.44
  1955.3 60.0 reduce-scatter.28
  2019.9 68.2 reduce-scatter.26
  2092.5 68.1 reduce-scatter.30
  2164.8 162.5 reduce-scatter.32
  2331.2 162.3 reduce-scatter.34
  2496.8 22.3 reduce-scatter.22
  2522.1 23.2 reduce-scatter.24
where the time goes:
time: 2570 us; the launch traced here: 2550 us
  waiting for transfers between devices  1440 us (56%)
  matrix products  314 us (12%)
  other arithmetic  295 us (11%)
  blocking collectives  198 us (8%)
  local copies, waits for them, and re-layouts  147 us (6%)
  starting transfers between devices  117 us (5%)
  loops' own time  31.6 us (1%)
    ppermute x14, waiting for transfers between devices, from_behind(): lax.ppermute(value, axis, [(source, source + steps) for source in range(l...  399 us
    unnamed x21, waiting for transfers between devices  264 us
    reduce_scatter x1, waiting for transfers between devices, body(): lax.psum_scatter(sums[7].astype(jnp.bfloat16), 'dp', scatter_dimension=1,...  165 us
    reduce_scatter x1, waiting for transfers between devices, body(): lax.psum_scatter(sums[9].astype(jnp.bfloat16), 'dp', scatter_dimension=1,...  163 us
    all_gather x1, waiting for transfers between devices, body(): lax.all_gather(shards[9], 'dp', axis=1, tiled=True)  138 us
    add x28, other arithmetic, add_trees(): left_val + right_val  125 us
    ppermute x14, starting transfers between devices, from_behind(): lax.ppermute(value, axis, [(source, source + steps) for source in range(l...  116 us
    reduce_scatter x1, waiting for transfers between devices, body(): lax.psum_scatter(sums[3].astype(jnp.bfloat16), 'dp', scatter_dimension=1,...  71.4 us
  transfers between devices with their start and end apart: 30, of which 21 were waited for; matrix products, arithmetic and copies ran while one was open for 3% of the time, Pallas kernels for 0%

commit v1 on v0

v1 whole, which is shorter than its diff:
```python
import math

import jax
import jax.numpy as jnp
from jax import lax
from jax.experimental import pallas as pl
from jax.experimental.pallas import tpu as pltpu
from jax.sharding import PartitionSpec as P

D = 768
HEADS = 12
HEAD_DIM = 64
ROT_DIM = 16
FF = 3072
PAIRS = HEADS // 2
LANES = 128
TILE = 256

EPSILON = 1e-05
ROPE_BASE = 10000.0
POSITION_SCALE = 4.0
NEG_FILL = -1e30
SCALE = 1.0 / math.sqrt(HEAD_DIM)
LOG2E = math.log2(math.e)
PRM_ROWS = 16
VMEM_BYTES = 30 * 1024 * 1024
Q_UNROLL, A_UNROLL, U_UNROLL, O_UNROLL, L_UNROLL = 3, 6, 12, 3, 1

F32 = jnp.float32
BF16 = jnp.bfloat16


def place_of(section):
    column, which = section // 2, section % 2
    return column, (which if column % 2 == 0 else 1 - which)


def send(value, rule):
    pipe_count, dp_count = lax.axis_size("pipe"), lax.axis_size("dp")
    half = dp_count // 2
    pairs = []
    for h in range(2):
        for r in range(half):
            for i in range(pipe_count // 2):
                for c in range(2):
                    target = rule(h, r, i, c)
                    if target is not None:
                        th, tr, ti, tc = target
                        pairs.append(
                            (
                                (h * half + r) * pipe_count + 2 * i + c,
                                (th * half + tr) * pipe_count + 2 * ti + tc,
                            )
                        )
    return lax.ppermute(value, ("dp", "pipe"), pairs)


def swap_core(h, r, i, c):
    return h, r, i, 1 - c


def swap_half(h, r, i, c):
    return 1 - h, r, i, c


def swap_bit(bit):
    return lambda h, r, i, c: (h, r ^ bit, i, c)


def to_stage(step, stage_count):
    def rule(h, r, i, c):
        for stage in range(stage_count):
            if place_of(stage) == (i, h) and 0 <= stage + step < stage_count:
                ti, th = place_of(stage + step)
                return th, r, ti, c
        return None

    return rule


def nn(left, right):
    return lax.dot_general(left, right, (((1,), (0,)), ((), ())), preferred_element_type=F32)


def nt(left, right):
    return lax.dot_general(left, right, (((1,), (1,)), ((), ())), preferred_element_type=F32)


def tn(left, right):
    return lax.dot_general(left, right, (((0,), (0,)), ((), ())), preferred_element_type=F32)


def spin(values, cos_t, low_t, high_t):
    return values * cos_t + pltpu.roll(values, LANES - 8, 1) * low_t + pltpu.roll(values, 8, 1) * high_t


def unspin(values, cos_t, low_t, high_t):
    return values * cos_t - pltpu.roll(values, LANES - 8, 1) * low_t - pltpu.roll(values, 8, 1) * high_t


def doubled_keys(kv_low):
    kv = kv_low.astype(F32)
    lane = lax.broadcasted_iota(jnp.int32, kv.shape, 1)
    other = pltpu.roll(kv, HEAD_DIM, 1)
    zero = jnp.zeros_like(kv)
    keys = jnp.concatenate(
        [jnp.where(lane < HEAD_DIM, kv, zero), jnp.where(lane < HEAD_DIM, zero, other)], axis=0
    ).astype(BF16)
    vals = jnp.concatenate(
        [jnp.where(lane < HEAD_DIM, other, zero), jnp.where(lane < HEAD_DIM, zero, kv)], axis=0
    ).astype(BF16)
    return keys, vals


def gelu_parts(values):
    size = jnp.abs(values)
    bell = jnp.exp2(values * values * (-0.5 * LOG2E))
    t = 1.0 / (1.0 + (0.3275911 / math.sqrt(2.0)) * size)
    poly = 0.5 * 1.061405429
    for coef in (-1.453152027, 1.421413741, -0.284496736, 0.254829592):
        poly = poly * t + 0.5 * coef
    tail = poly * t * bell
    share = jnp.where(values >= 0.0, 1.0 - tail, tail)
    return values * share, share + values * (bell * (1.0 / math.sqrt(2.0 * math.pi)))


def fetch(source, target, sem):
    pltpu.make_async_copy(source, target, sem).start()


def landed(target, sem):
    pltpu.make_async_copy(target, target, sem).wait()


def pack_kernel(*refs):
    wq, wo, wu, wd, kvw, gain, shift, bias, kv_bias, up_bias = refs[:10]
    out_a, out_b, part_a, part_b, small, in_sems, out_sem = refs[10:]
    width, wide = wq.shape[1], wd.shape[1]
    body_rows = width + wide
    for layer in range(2):
        at = layer * body_rows
        for k in range(FF // D):
            fetch(
                wu.at[layer, :, pl.ds(k * D, D)], part_b.at[pl.ds(at + k * width, width)], in_sems.at[2 * layer + 1]
            )
        fetch(wo.at[layer], part_b.at[pl.ds(at + wide, width)], in_sems.at[2 * layer + 1])
    for layer in range(2):
        at = layer * body_rows
        fetch(wd.at[layer], part_a.at[pl.ds(at, wide)], in_sems.at[2 * layer])
        fetch(wq.at[layer], part_a.at[pl.ds(at + wide, width)], in_sems.at[2 * layer])
    last = pl.ds(2 * body_rows, 16)
    for k in range(width // 16):
        fetch(kvw.at[0, pl.ds(16 * k, 16)], part_a.at[last, pl.ds(k * LANES, LANES)], in_sems.at[4])
    small[...] = jnp.zeros_like(small)
    row = 0
    for item in (gain, shift, bias):
        for layer in range(2):
            for k in range(item.shape[1]):
                small[row : row + 1, :width] = item[layer, k : k + 1, :].astype(F32)
                row += 1
    small[row : row + 1, : kv_bias.shape[1]] = kv_bias[...].astype(F32)
    for layer in range(2):
        small[row + 1 : row + 2, layer * wide : (layer + 1) * wide] = up_bias[layer : layer + 1, :].astype(F32)
    for layer in range(2):
        landed(part_b.at[pl.ds(layer * body_rows, body_rows)], in_sems.at[2 * layer + 1])
    part_b[last, :] = small[...].astype(BF16)
    fetch(part_b, out_b, out_sem.at[0])
    for layer in range(2):
        landed(part_a.at[pl.ds(layer * body_rows, body_rows)], in_sems.at[2 * layer])
    landed(part_a.at[last], in_sems.at[4])
    fetch(part_a, out_a, out_sem.at[1])
    landed(out_b, out_sem.at[0])
    landed(out_a, out_sem.at[1])


def pack(w_query, w_output, w_up, w_down, w_keyval, small_items):
    width, wide = w_query.shape[1], w_down.shape[1]
    rows = 2 * (width + wide) + 16
    shape = pltpu.HBM((rows, D), BF16)
    return pl.pallas_call(
        pack_kernel,
        out_shape=[shape, shape],
        in_specs=any_specs(5) + [pl.BlockSpec(memory_space=pltpu.VMEM)] * 5,
        out_specs=[pl.BlockSpec(memory_space=pltpu.HBM)] * 2,
        scratch_shapes=[pltpu.VMEM((rows, D), BF16)] * 2
        + [pltpu.VMEM((16, D), F32), pltpu.SemaphoreType.DMA((5,)), pltpu.SemaphoreType.DMA((2,))],
        compiler_params=pltpu.CompilerParams(vmem_limit_bytes=58 * 1024 * 1024),
        name="pack_shard",
    )(w_query, w_output, w_up, w_down, w_keyval, *small_items)


def gather_kernel(count, width, wide, *refs):
    half = count // 2
    pieces = count + 2
    sc, own, other = refs[0], refs[1 : 1 + pieces], refs[1 + pieces : 1 + 2 * pieces]
    wq, wo, wu, wd = refs[-5:-1]
    sems = refs[-1]

    def lay(first, second):
        for place in range(count):
            at = pl.multiple_of(sc[1 + place] * width, 16)
            wide_at = pl.multiple_of(sc[1 + place] * wide, 16)
            split = place % half == half - 1
            for layer in range(2):
                index = place + place // half + (layer if split else 0)
                part_a, part_b = first[index], second[index]
                start = 0 if split else layer * (width + wide)
                fetch(part_a.at[pl.ds(start, wide)], wd.at[layer, pl.ds(wide_at, wide)], sems.at[3])
                fetch(part_a.at[pl.ds(start + wide, width)], wq.at[layer, pl.ds(at, width)], sems.at[0])
                for k in range(FF // D):
                    fetch(
                        part_b.at[pl.ds(start + k * width, width)],
                        wu.at[layer, pl.ds(at, width), pl.ds(k * D, D)],
                        sems.at[2],
                    )
                fetch(part_b.at[pl.ds(start + wide, width)], wo.at[layer, pl.ds(at, width)], sems.at[1])

    pl.when(sc[0] == 1)(lambda: lay(own, other))
    pl.when(sc[0] == 0)(lambda: lay(other, own))
    for index, target in enumerate((wq, wo, wu, wd)):
        landed(target, sems.at[index])


def copy_kernel(*refs):
    sources, targets, sems = refs[:4], refs[-5:-1], refs[-1]
    for index, (source, target) in enumerate(zip(sources, targets)):
        fetch(source, target, sems.at[index])
    for index, target in enumerate(targets):
        landed(target, sems.at[index])


def resident(scalars, own, other, width, wide):
    if scalars is None:
        lead, sources, kernel = [], own, copy_kernel
    else:
        flat = lambda lines: [item for line in lines for item in line[:-1] + line[-1]]
        lead, sources = [scalars], flat(own) + flat(other)
        kernel = lambda *refs: gather_kernel(D // width, width, wide, *refs)
    return pl.pallas_call(
        kernel,
        out_shape=[pltpu.VMEM((2,) + shape, BF16) for shape in ((D, D), (D, D), (D, FF), (FF, D))],
        in_specs=[pl.BlockSpec(memory_space=pltpu.SMEM)] * len(lead) + any_specs(len(sources)),
        out_specs=[pl.BlockSpec(memory_space=pltpu.VMEM)] * 4,
        scratch_shapes=[pltpu.SemaphoreType.DMA((4,))],
        compiler_params=pltpu.CompilerParams(vmem_limit_bytes=1024 * 1024),
        name="gather_shards",
    )(*lead, *[pltpu.with_memory_space_constraint(item, pltpu.HBM) for item in sources])


def weight_grad_kernel(layer, count, *refs):
    sc = refs[0]
    inputs = refs[1:8]
    more = refs[8:10] if layer == 0 else ()
    place = 8 + len(more)
    kept, given = refs[place : place + count], refs[place + count : place + 2 * count]
    scratch = refs[place + 2 * count :]
    held, part_a, part_b = scratch[:7], scratch[7], scratch[8]
    extra = scratch[9 : 9 + len(more)]
    in_sem, out_sem = scratch[-2:]
    g, d, u, m, a, q, o = held
    for index, (source, target) in enumerate(zip(inputs, held)):
        fetch(source, target, in_sem.at[index])
    width, wide = D // count, FF // count
    rows = g.shape[0]
    if more:
        fetch(more[0], extra[0], in_sem.at[7])
        fetch(more[1], part_b.at[:, pl.ds(width + wide, 16)], in_sem.at[8])
    landed(g, in_sem.at[0])
    landed(d, in_sem.at[1])
    for shard in range(count):
        cols = slice(shard * wide, (shard + 1) * wide)
        part_a[shard, :wide, :] = tn(g[:, cols], d[...]).astype(BF16)
    landed(u, in_sem.at[2])
    landed(m, in_sem.at[3])
    for k in range(FF // D):
        block = tn(m[...], u[:, k * D : (k + 1) * D]).astype(BF16)
        for shard in range(count):
            part_b[shard, k * width : (k + 1) * width, :] = block[shard * width : (shard + 1) * width]
    landed(a, in_sem.at[4])
    landed(q, in_sem.at[5])
    block = tn(a[...], q[...]).astype(BF16)
    for shard in range(count):
        part_a[shard, wide : wide + width, :] = block[shard * width : (shard + 1) * width]
    landed(o, in_sem.at[6])
    block = tn(o[...], d[...]).astype(BF16)
    for shard in range(count):
        part_b[shard, wide : wide + width, :] = block[shard * width : (shard + 1) * width]
    if more:
        landed(extra[0], in_sem.at[7])
        block = tn(a[...], extra[0][...]).astype(BF16)
        for shard in range(count):
            for k in range(width // 16):
                start = shard * width + 16 * k
                part_a[shard, width + wide :, k * LANES : (k + 1) * LANES] = block[start : start + 16]
        landed(part_b.at[:, pl.ds(width + wide, 16)], in_sem.at[8])

    def leave(first, second):
        for j in range(count):
            fetch(first.at[sc[1 + j]], kept[j], out_sem.at[j])
            fetch(second.at[sc[1 + j]], given[j], out_sem.at[count + j])

    pl.when(sc[0] == 1)(lambda: leave(part_a, part_b))
    pl.when(sc[0] == 0)(lambda: leave(part_b, part_a))
    for j in range(count):
        landed(kept[j], out_sem.at[j])
        landed(given[j], out_sem.at[count + j])


def weight_grads(scalars, inputs, more, layer, count):
    rows = inputs[0].shape[0]
    part_rows = (D + FF) // count + (16 if more else 0)
    part = pltpu.HBM((part_rows, D), BF16)
    flops = 4 * rows * D * (D + FF)
    results = pl.pallas_call(
        lambda *refs: weight_grad_kernel(layer, count, *refs),
        out_shape=[part] * (2 * count),
        in_specs=[pl.BlockSpec(memory_space=pltpu.SMEM)] + any_specs(7 + len(more)),
        out_specs=[pl.BlockSpec(memory_space=pltpu.HBM)] * (2 * count),
        scratch_shapes=[pltpu.VMEM(item.shape, BF16) for item in inputs]
        + [pltpu.VMEM((count, part_rows, D), BF16)] * 2
        + [pltpu.VMEM(item.shape, BF16) for item in more[:1]]
        + [pltpu.SemaphoreType.DMA((9,)), pltpu.SemaphoreType.DMA((2 * count,))],
        compiler_params=pltpu.CompilerParams(vmem_limit_bytes=58 * 1024 * 1024),
        cost_estimate=pl.CostEstimate(flops=flops, bytes_accessed=22_000_000, transcendentals=0),
        name="weight_grads",
    )(scalars, *inputs, *more)
    return results[:count], results[count:]


FWD_STASH = ("a", "m", "o", "q", "n", "g", "w", "p", "r")


def span(index, size):
    return pl.ds(pl.multiple_of(index * size, size), size)


def loop(count, unroll, step):
    def body(index, carry):
        step(index)
        return carry

    lax.fori_loop(0, count, body, 0, unroll=unroll)


def forward_kernel(tick, micro_count, *refs):
    sc, prm_h, tab_h, kvw_h, fresh_h, inc_h, wq, wo, wu, wd = refs[:10]
    place = 10 if tick == 0 else 10 + 20
    y_h, ys_h = refs[place : place + 2]
    stash_h = refs[place + 2 : place + 21]
    (
        kvw, prm, tab, xin, yout, s_a, s_m, s_o, s_q, s_n, s_g, s_w, s_p, s_r, s_kv, s_x, s_keys, s_vals,
        in_sem, out_sem,
    ) = refs[place + 21 :]
    stage = sc[0]
    slot = tick - 2 * stage
    rows = xin.shape[0]

    @pl.when((slot >= 0) & (slot < micro_count))
    def work():
        @pl.when(stage == 0)
        def take_fresh():
            fetch(fresh_h.at[slot], xin, in_sem.at[0])

        @pl.when(stage != 0)
        def take_sent():
            fetch(inc_h, xin, in_sem.at[0])

        fetch(prm_h, prm, in_sem.at[1])
        fetch(tab_h.at[slot], tab, in_sem.at[2])
        fetch(kvw_h, kvw, in_sem.at[3])
        landed(xin, in_sem.at[0])
        landed(prm, in_sem.at[1])
        landed(tab, in_sem.at[2])
        landed(kvw, in_sem.at[3])
        s_x[...] = xin[...].astype(F32)
        sources = (s_a, s_m, s_o, s_q, s_n, s_g, s_w, s_p, s_r)

        def kept(layer, index):
            number = 9 * layer + index
            return pltpu.make_async_copy(
                sources[index].at[layer], stash_h[number].at[slot], out_sem.at[number]
            )

        def keep(layer, index):
            for fixed in range(2):
                pl.when(layer == fixed)(lambda: kept(fixed, index).start())

        def one_layer(layer):
            x = s_x[...]
            row_of = lambda number: prm[layer, number : number + 1, :]
            mean = jnp.mean(x, axis=1, keepdims=True)
            centred = x - mean
            rstd = lax.rsqrt(jnp.mean(centred * centred, axis=1, keepdims=True) + EPSILON)
            normed = centred * rstd
            s_n[layer] = normed.astype(BF16)
            s_r[layer] = jnp.broadcast_to(rstd, (rows, LANES))
            s_a[layer] = (normed * row_of(0) + row_of(2)).astype(BF16)
            s_m[layer] = (normed * row_of(1) + row_of(3)).astype(BF16)
            for index in (0, 1, 4, 8):
                keep(layer, index)

            def query_tile(n):
                cols = span(n, TILE)
                q_lin = nn(s_a[layer], wq[layer, :, cols]) + prm[layer, 4:5, cols]
                turned = [
                    spin(q_lin[:, k * LANES : (k + 1) * LANES], tab[0], tab[1], tab[2])
                    for k in range(TILE // LANES)
                ]
                s_q[layer, :, cols] = jnp.concatenate(turned, axis=1).astype(BF16)

            loop(D // TILE, Q_UNROLL, query_tile)
            keep(layer, 3)

            @pl.when(layer == 0)
            def make_keys():
                col = lax.broadcasted_iota(jnp.int32, (rows, LANES), 1)
                kv_lin = nn(s_a[0], kvw[...]) + prm[0, 10:11, :LANES]
                s_kv[...] = jnp.where(
                    col < HEAD_DIM, spin(kv_lin, tab[0], tab[1], tab[2]), kv_lin
                ).astype(BF16)
                pltpu.make_async_copy(s_kv, stash_h[18].at[slot], out_sem.at[18]).start()
                s_keys[...], s_vals[...] = doubled_keys(s_kv[...])

            def attend(pair):
                cols = span(pair, LANES)
                row = lax.broadcasted_iota(jnp.int32, (rows, LANES), 0)
                col = lax.broadcasted_iota(jnp.int32, (rows, LANES), 1)
                scores = nt(s_q[layer, :, cols], s_keys[...]) * (SCALE * LOG2E)
                halves = []
                for side in range(2):
                    one = scores[:, side * LANES : (side + 1) * LANES]
                    one = jnp.where(row >= col, one, NEG_FILL)
                    raised = jnp.exp2(one - jnp.max(one, axis=1, keepdims=True))
                    halves.append(raised * (1.0 / jnp.sum(raised, axis=1, keepdims=True)))
                probs = jnp.concatenate(halves, axis=1).astype(BF16)
                s_p[layer, span(pair, rows), :] = probs
                s_o[layer, :, cols] = nn(probs, s_vals[...]).astype(BF16)

            loop(PAIRS, A_UNROLL, attend)
            keep(layer, 2)
            keep(layer, 7)

            def up_tile(n):
                cols = span(n, TILE)
                bias = prm[layer, pl.ds(6 + n // (D // TILE), 1), span(n % (D // TILE), TILE)]
                pre = nn(s_m[layer], wu[layer, :, cols]) + bias
                act, slope = gelu_parts(pre)
                s_g[layer, :, cols] = act.astype(BF16)
                s_w[layer, :, cols] = slope.astype(BF16)

            loop(FF // TILE, U_UNROLL, up_tile)
            keep(layer, 5)
            keep(layer, 6)

            def out_tile(n):
                cols = span(n, TILE)
                s_x[:, cols] = (
                    s_x[:, cols]
                    + nn(s_o[layer], wo[layer, :, cols])
                    + nn(s_g[layer], wd[layer, :, cols])
                    + prm[layer, 5:6, cols]
                )

            loop(D // TILE, O_UNROLL, out_tile)

        loop(2, L_UNROLL, one_layer)
        yout[...] = s_x[...].astype(BF16)
        last = [
            pltpu.make_async_copy(yout, y_h, out_sem.at[19]),
            pltpu.make_async_copy(yout, ys_h.at[slot], out_sem.at[20]),
        ]
        for copy in last:
            copy.start()
        for layer in range(2):
            for index in range(9):
                kept(layer, index).wait()
        pltpu.make_async_copy(s_kv, stash_h[18].at[slot], out_sem.at[18]).wait()
        for copy in last:
            copy.wait()


def backward_kernel(tick, micro_count, stage_count, *refs):
    sc, prm_h, tab_h, kvw_h, cot_h, inc_h, wq, wo, wu, wd = refs[:10]
    place = 10
    stash_h = refs[place : place + 11]
    place += 11 if tick == 0 else 11 + 9
    x_h, xs_h = refs[place : place + 2]
    outs_h = refs[place + 2 : place + 10]
    (
        kvw, prm, tab, din, dout, t_q, t_n, t_w, t_p, t_r, t_kv,
        s_d, s_u, s_q, s_kv, s_sum, d_mix, d_a, d_m, s_y, s_keys, s_vals, s_dk, s_dv, s_dkv,
        in_sem, st_sem, out_sem,
    ) = refs[place + 10 :]
    stage = sc[0]
    slot = tick - 2 * (stage_count - 1 - stage)
    rows = din.shape[0]

    @pl.when((slot >= 0) & (slot < micro_count))
    def work():
        @pl.when(stage == stage_count - 1)
        def take_given():
            fetch(cot_h.at[slot], din, in_sem.at[0])

        @pl.when(stage != stage_count - 1)
        def take_sent():
            fetch(inc_h, din, in_sem.at[0])

        fetch(prm_h, prm, in_sem.at[1])
        fetch(tab_h.at[slot], tab, in_sem.at[2])
        fetch(kvw_h, kvw, in_sem.at[3])
        fetch(stash_h[10].at[slot], t_kv, in_sem.at[4])
        for layer in (1, 0):
            for index, target in ((2, t_w), (3, t_p), (0, t_q), (1, t_n), (4, t_r)):
                fetch(stash_h[5 * layer + index].at[slot], target.at[layer], st_sem.at[layer, index])
        landed(din, in_sem.at[0])
        landed(prm, in_sem.at[1])
        landed(tab, in_sem.at[2])
        landed(kvw, in_sem.at[3])
        landed(t_kv, in_sem.at[4])
        s_y[...] = din[...].astype(F32)
        s_keys[...], s_vals[...] = doubled_keys(t_kv[...])
        s_sum[...] = jnp.zeros_like(s_sum)
        s_dkv[...] = jnp.zeros_like(s_dkv)
        sources = (s_d, s_u, s_q)

        def kept(layer, index):
            number = 3 * layer + index
            return pltpu.make_async_copy(
                sources[index].at[layer], outs_h[number].at[slot], out_sem.at[number]
            )

        def keep(layer, index):
            for fixed in range(2):
                pl.when(layer == fixed)(lambda: kept(fixed, index).start())

        def one_layer(turn):
            layer = 1 - turn
            lane = lax.broadcasted_iota(jnp.int32, (rows, LANES), 1)
            s_d[layer] = s_y[...].astype(BF16)
            keep(layer, 0)
            s_sum[layer, 5:6, :] = jnp.sum(s_d[layer].astype(F32), axis=0, keepdims=True)
            landed(t_w.at[layer], st_sem.at[layer, 2])

            def act_tile(n):
                cols = span(n, TILE)
                d_act = nt(s_d[layer], wd[layer, cols, :])
                d_pre = (d_act * t_w[layer, :, cols].astype(F32)).astype(BF16)
                s_u[layer, :, cols] = d_pre
                s_sum[layer, pl.ds(6 + n // (D // TILE), 1), span(n % (D // TILE), TILE)] = jnp.sum(
                    d_pre.astype(F32), axis=0, keepdims=True
                )

            loop(FF // TILE, U_UNROLL, act_tile)
            keep(layer, 1)

            def mix_tile(n):
                cols = span(n, TILE)
                d_mix[:, cols] = nt(s_d[layer], wo[layer, cols, :]).astype(BF16)
                d_m[:, cols] = nt(s_u[layer], wu[layer, cols, :])

            loop(D // TILE, O_UNROLL, mix_tile)
            landed(t_p.at[layer], st_sem.at[layer, 3])
            landed(t_q.at[layer], st_sem.at[layer, 0])
            s_dv[...] = jnp.zeros_like(s_dv)
            s_dk[...] = jnp.zeros_like(s_dk)

            def attend(pair):
                cols = span(pair, LANES)
                probs_low = t_p[layer, span(pair, rows), :]
                probs = probs_low.astype(F32)
                d_one = d_mix[:, cols]
                d_probs = nt(d_one, s_vals[...])
                halves = []
                for side in range(2):
                    part = slice(side * LANES, (side + 1) * LANES)
                    weighed = d_probs[:, part] * probs[:, part]
                    dot_row = jnp.sum(weighed, axis=1, keepdims=True)
                    halves.append(weighed - probs[:, part] * dot_row)
                d_scores = jnp.concatenate(halves, axis=1).astype(BF16)
                d_q = unspin(nn(d_scores, s_keys[...]) * SCALE, tab[0], tab[1], tab[2])
                s_q[layer, :, cols] = d_q.astype(BF16)
                s_dv[...] += tn(probs_low, d_one)
                s_dk[...] += tn(d_scores, t_q[layer, :, cols])

            loop(PAIRS, A_UNROLL, attend)
            keep(layer, 2)
            s_sum[layer, 4:5, :] = jnp.sum(s_q[layer].astype(F32), axis=0, keepdims=True)
            s_dkv[...] += jnp.where(
                lane < HEAD_DIM,
                (s_dk[:rows, :] + pltpu.roll(s_dk[rows:, :], HEAD_DIM, 1)) * SCALE,
                pltpu.roll(s_dv[:rows, :], HEAD_DIM, 1) + s_dv[rows:, :],
            )

            def back_tile(n):
                cols = span(n, TILE)
                d_a[:, cols] = nt(s_q[layer], wq[layer, cols, :])

            loop(D // TILE, Q_UNROLL, back_tile)

            @pl.when(layer == 0)
            def through_keys():
                total = s_dkv[...]
                turned = jnp.where(lane < HEAD_DIM, unspin(total, tab[0], tab[1], tab[2]), total)
                s_kv[...] = turned.astype(BF16)
                pltpu.make_async_copy(s_kv, outs_h[6].at[slot], out_sem.at[6]).start()
                s_sum[0, 10:11, :LANES] = jnp.sum(s_kv[...].astype(F32), axis=0, keepdims=True)
                d_a[...] += nt(s_kv[...], kvw[...])

            landed(t_n.at[layer], st_sem.at[layer, 1])
            landed(t_r.at[layer], st_sem.at[layer, 4])
            normed = t_n[layer].astype(F32)
            da, dm = d_a[...], d_m[...]
            s_sum[layer, 0:1, :] = jnp.sum(da * normed, axis=0, keepdims=True)
            s_sum[layer, 1:2, :] = jnp.sum(dm * normed, axis=0, keepdims=True)
            s_sum[layer, 2:3, :] = jnp.sum(da, axis=0, keepdims=True)
            s_sum[layer, 3:4, :] = jnp.sum(dm, axis=0, keepdims=True)
            d_normed = da * prm[layer, 0:1, :] + dm * prm[layer, 1:2, :]
            mean_one = jnp.mean(d_normed, axis=1, keepdims=True)
            mean_two = jnp.mean(d_normed * normed, axis=1, keepdims=True)
            s_y[...] += t_r[layer, :, 0:1] * (d_normed - mean_one - normed * mean_two)

        loop(2, L_UNROLL, one_layer)
        dout[...] = s_y[...].astype(BF16)
        last = [
            pltpu.make_async_copy(s_sum, outs_h[7].at[slot], out_sem.at[7]),
            pltpu.make_async_copy(dout, x_h, out_sem.at[8]),
            pltpu.make_async_copy(dout, xs_h.at[slot], out_sem.at[9]),
        ]
        for copy in last:
            copy.start()
        for layer in range(2):
            for index in range(3):
                kept(layer, index).wait()
        pltpu.make_async_copy(s_kv, outs_h[6].at[slot], out_sem.at[6]).wait()
        for copy in last:
            copy.wait()


def any_specs(how_many):
    return [pl.BlockSpec(memory_space=pl.ANY)] * how_many


def in_vmem(values):
    return [pltpu.with_memory_space_constraint(value, pltpu.VMEM) for value in values]


def call_tick(kernel, name, operands, carried, weight_count, scratch, rows):
    shapes = [jax.ShapeDtypeStruct((rows, D), BF16)] + [
        jax.ShapeDtypeStruct(item.shape, item.dtype) for item in carried
    ]
    carried = [item for item in carried if not isinstance(item, jax.ShapeDtypeStruct)]
    first_carried = len(operands)
    operands = operands + carried
    vmem = [pl.BlockSpec(memory_space=pltpu.VMEM)] * weight_count
    return pl.pallas_call(
        kernel,
        out_shape=shapes,
        in_specs=[pl.BlockSpec(memory_space=pltpu.SMEM)]
        + any_specs(5)
        + vmem
        + any_specs(len(operands) - 6 - weight_count),
        out_specs=any_specs(len(shapes)),
        input_output_aliases={first_carried + k: 1 + k for k in range(len(carried))},
        scratch_shapes=scratch,
        compiler_params=pltpu.CompilerParams(vmem_limit_bytes=VMEM_BYTES),
        cost_estimate=pl.CostEstimate(
            flops=4 * rows * D * (D + FF) * 2, bytes_accessed=10_000_000, transcendentals=0
        ),
        name=name,
    )(*operands)


def shared_scratch(rows):
    return [
        pltpu.VMEM((D, LANES), BF16),
        pltpu.VMEM((2, PRM_ROWS, D), F32),
        pltpu.VMEM((3, rows, LANES), F32),
        pltpu.VMEM((rows, D), BF16),
        pltpu.VMEM((rows, D), BF16),
    ]


def forward_tick(tick, scalars, fixed, given, incoming, weights, ys, stash, rows):
    micro_count = ys.shape[0]
    scratch = shared_scratch(rows) + [
        *[pltpu.VMEM((2, rows, D), BF16) for _ in range(5)],
        pltpu.VMEM((2, rows, FF), BF16),
        pltpu.VMEM((2, rows, FF), BF16),
        pltpu.VMEM((2, PAIRS * rows, 2 * LANES), BF16),
        pltpu.VMEM((2, rows, LANES), F32),
        pltpu.VMEM((rows, LANES), BF16),
        pltpu.VMEM((rows, D), F32),
        pltpu.VMEM((2 * rows, LANES), BF16),
        pltpu.VMEM((2 * rows, LANES), BF16),
        pltpu.SemaphoreType.DMA((4,)),
        pltpu.SemaphoreType.DMA((21,)),
    ]
    results = call_tick(
        lambda *refs: forward_kernel(tick, micro_count, *refs),
        "forward_tick",
        [scalars, *fixed, given, incoming, *in_vmem(weights)],
        [ys, *stash],
        len(weights),
        scratch,
        rows,
    )
    return results[0], results[1], list(results[2:])


def backward_tick(tick, stage_count, scalars, fixed, given, incoming, weights, stash, xs, outs, rows):
    micro_count = xs.shape[0]
    scratch = shared_scratch(rows) + [
        pltpu.VMEM((2, rows, D), BF16),
        pltpu.VMEM((2, rows, D), BF16),
        pltpu.VMEM((2, rows, FF), BF16),
        pltpu.VMEM((2, PAIRS * rows, 2 * LANES), BF16),
        pltpu.VMEM((2, rows, LANES), F32),
        pltpu.VMEM((rows, LANES), BF16),
        pltpu.VMEM((2, rows, D), BF16),
        pltpu.VMEM((2, rows, FF), BF16),
        pltpu.VMEM((2, rows, D), BF16),
        pltpu.VMEM((rows, LANES), BF16),
        pltpu.VMEM((2, PRM_ROWS, D), F32),
        pltpu.VMEM((rows, D), BF16),
        pltpu.VMEM((rows, D), F32),
        pltpu.VMEM((rows, D), F32),
        pltpu.VMEM((rows, D), F32),
        pltpu.VMEM((2 * rows, LANES), BF16),
        pltpu.VMEM((2 * rows, LANES), BF16),
        pltpu.VMEM((2 * rows, LANES), F32),
        pltpu.VMEM((2 * rows, LANES), F32),
        pltpu.VMEM((rows, LANES), F32),
        pltpu.SemaphoreType.DMA((5,)),
        pltpu.SemaphoreType.DMA((2, 5)),
        pltpu.SemaphoreType.DMA((10,)),
    ]
    results = call_tick(
        lambda *refs: backward_kernel(tick, micro_count, stage_count, *refs),
        "backward_tick",
        [scalars, *fixed, given, incoming, *in_vmem(weights), *stash],
        [xs, *outs],
        len(weights),
        scratch,
        rows,
    )
    return results[0], results[1], list(results[2:])


def rotary_tables(positions):
    half_width = ROT_DIM // 2
    inverse = ROPE_BASE ** (-2.0 * jnp.arange(half_width, dtype=F32) / ROT_DIM)
    angles = (positions.astype(F32) / POSITION_SCALE)[..., None] * inverse
    cosine, sine = jnp.cos(angles), jnp.sin(angles)
    rest = jnp.ones(angles.shape[:-1] + (HEAD_DIM - ROT_DIM,), F32)
    blank = jnp.zeros_like(cosine)
    cos_t = jnp.concatenate([cosine, cosine, rest] * 2, axis=-1)
    low_t = jnp.concatenate([-sine, blank, 0.0 * rest] * 2, axis=-1)
    high_t = jnp.concatenate([blank, sine, 0.0 * rest] * 2, axis=-1)
    return jnp.stack([cos_t, low_t, high_t], axis=-3)


def after(values, done):
    kept, unused = lax.optimization_barrier((tuple(values), tuple(done)))
    return list(kept)


def spread(part_a, part_b, native, half, tail_rows, before, beside, use_tails, late):
    side = lambda value: send(value, swap_bit(1))
    up = lambda value: send(value, swap_bit(2))
    core = lambda value: send(value, swap_core)
    received = core(part_b)
    here, away = jnp.where(native, part_a, received), jnp.where(native, received, part_a)
    move = lambda value: send(value, swap_half)
    if half != 4:
        own, other = [], []
        for start in (here, move(away)):
            line = [start]
            for mask in range(1, half):
                bit = mask & -mask
                line.append(send(line[mask ^ bit], swap_bit(bit)))
            own.append(line)
            other.append([core(value) for value in line])
        tails = [[item[-tail_rows:] for line in lines for item in line] for lines in (own, other)]
        return own, other, use_tails(*tails), late([])

    here, away = after([here, away], before)
    m0, n1, n2 = move(away), side(here), up(here)
    c0 = core(here)
    m0, n1, n2, c0 = after([m0, n1, n2, c0], [m0, n1, n2, c0] + beside)
    cut = (m0.shape[0] - tail_rows) // 2
    m1, m2 = side(m0), up(m0)
    n3 = [up(n1[:cut]), side(n2[cut:])]
    far_tail = send(m0[-tail_rows:], swap_bit(3))
    c1, c2, k0 = (core(value) for value in (n1, n2, m0))
    m1, m2, c1, c2, k0, far_tail, *n3 = after(
        [m1, m2, c1, c2, k0, far_tail, *n3], [m1, m2, c1, c2, k0, far_tail, *n3]
    )
    m3 = [up(m1[:cut]), side(m2[cut:])]
    k1, k2, far_other = core(m1), core(m2), core(far_tail)
    c3 = [core(value) for value in n3]
    late_done = late([k1])
    tails = [
        [item[-tail_rows:] for item in (*line, far)]
        for line, far in (((here, n1, n2, n3[1], m0, m1, m2), far_tail), ((c0, c1, c2, c3[1], k0, k1, k2), far_other))
    ]
    made = use_tails(*tails)
    m3 = after(m3, [*m3, k1, k2, *c3, *made])
    k3 = [core(value) for value in m3]
    own = [[here, n1, n2, n3], [m0, m1, m2, m3]]
    other = [[c0, c1, c2, c3], [k0, k1, k2, k3]]
    return own, other, made, late_done


def add_low(left, right):
    return (left.astype(F32) + right.astype(F32)).astype(BF16)


def reduce_home(make_parts, native, half, ended):
    side = lambda value: send(value, swap_bit(1))
    up = lambda value: send(value, swap_bit(2))
    core = lambda value: send(value, swap_core)
    move = lambda value: send(value, swap_half)

    def chip_sums(parts):
        kept, given = parts
        received = [[core(value) for value in line] for line in reversed(given)][::-1]
        return [[add_low(x, y) for x, y in zip(*lines)] for lines in zip(kept, received)]

    def finish(kept, moved):
        first = jnp.where(native, kept, moved)
        return first, core(jnp.where(native, moved, kept))

    if half != 4:
        results = []
        for layer in range(2):
            sums = chip_sums(make_parts(layer, []))
            for kind in range(2):
                bit = half // 2
                while bit:
                    for mask in range(bit):
                        sums[kind][mask] = add_low(sums[kind][mask], send(sums[kind][mask + bit], swap_bit(bit)))
                    bit //= 2
            results.append(finish(sums[0][0], move(sums[1][0])))
        return results

    n1, m1 = chip_sums(make_parts(1, []))
    s1, s3 = side(m1[1]), side(m1[3])
    n0, m0 = chip_sums(make_parts(0, ended))
    t2, t3 = up(m0[2]), up(m0[3])
    m1_0, m1_2 = add_low(m1[0], s1), add_low(m1[2], s3)
    m0_0, m0_1 = add_low(m0[0], t2), add_low(m0[1], t3)
    m1_2, m0_1 = after([m1_2, m0_1], [s1, s3, t2, t3])
    s2, t1 = up(m1_2), side(m0_1)
    m1_0, m0_0, *late = after([add_low(m1_0, s2), add_low(m0_0, t1), n1[1], n1[3], n0[1], n0[3]], [s2, t1])
    moved1, moved0 = move(m1_0), move(m0_0)
    a1, a3, b1, b3 = (side(value) for value in late)
    n1_0, n1_2 = add_low(n1[0], a1), add_low(n1[2], a3)
    n0_0, n0_2 = add_low(n0[0], b1), add_low(n0[2], b3)
    n1_0 = add_low(n1_0, up(n1_2))
    n0_0 = add_low(n0_0, up(n0_2))
    return [finish(n0_0, moved0), finish(n1_0, moved1)]


def pad_rows(flat, unit):
    short = -flat.shape[-1] % unit
    return jnp.pad(flat, [(0, 0)] * (flat.ndim - 1) + [(0, short)])


def body(
    inputs,
    out_cotangent,
    positions,
    norm_gain,
    norm_bias,
    row_bias,
    w_query,
    w_keyval,
    keyval_bias,
    w_output,
    w_up,
    up_bias,
    w_down,
):
    stage_count = lax.axis_size("pipe")
    replicas = lax.axis_size("dp")
    half = replicas // 2
    pipe_at, dp_at = lax.axis_index("pipe"), lax.axis_index("dp")
    column, core = pipe_at // 2, pipe_at % 2
    upper, replica = dp_at // half, dp_at % half
    stage = 2 * column + jnp.where(column % 2 == 0, upper, 1 - upper)
    micro_count, row_part = inputs.shape[:2]
    rows = row_part * stage_count
    width = D // replicas
    wide = FF // replicas

    (first_i, first_h), (last_i, last_h) = place_of(0), place_of(stage_count - 1)
    turn = stage_count // 2

    def whole_rows(entering, ending):
        starts, ends = [None] * stage_count, [None] * stage_count
        for source in range(stage_count):
            opposite = (source + turn) % stage_count

            def rule(h, r, i, c):
                if 2 * i + c == source:
                    return first_h, r, first_i, h
                return (last_h, r, last_i, h) if 2 * i + c == opposite else None

            part = send(jnp.where(pipe_at == source, entering, ending), rule)
            starts[source], ends[opposite] = part, part
        return jnp.concatenate(starts, axis=1), jnp.concatenate(ends, axis=1)

    def home_rows(leaving, started):
        final, grad = None, None
        for target in range(stage_count):
            opposite = (target + turn) % stage_count

            def rule(h, r, i, c):
                if (i, h) == (last_i, last_h):
                    return c, r, target // 2, target % 2
                return (c, r, opposite // 2, opposite % 2) if (i, h) == (first_i, first_h) else None

            rows_of = lambda value, at: value[:, at * row_part : (at + 1) * row_part]
            value = jnp.where(stage == stage_count - 1, rows_of(leaving, target), rows_of(started, opposite))
            part = send(value, rule)
            final = part if final is None else jnp.where(pipe_at == target, part, final)
            grad = part if grad is None else jnp.where(pipe_at == opposite, part, grad)
        return final, grad

    other_positions = send(positions, swap_half)
    tables = rotary_tables(jnp.where(core == upper, positions, other_positions))

    native = (column % 2 == 0) == (core == upper)
    small_items = (norm_gain, norm_bias, row_bias, keyval_bias, up_bias)
    kernels = width % 16 == 0 and half == 4
    body_rows = wide + width
    flat_rows = lambda item: pad_rows(item.reshape(-1), 16 * D).reshape(-1, D)
    small_shapes = [item.shape for item in small_items]
    small_counts = [4, 4, 6, 1, 1]
    if kernels:
        part_a, part_b = pack(w_query, w_output, w_up, w_down, w_keyval, small_items)
    else:
        lines = [item.reshape(count, -1) for item, count in zip(small_items, small_counts)]
        small_rows = jnp.concatenate([jnp.pad(line, ((0, 0), (0, D - line.shape[1]))) for line in lines])
        lines_a, lines_b = [], []
        for layer in range(2):
            lines_a += [w_down[layer], w_query[layer]]
            lines_b += [w_up[layer, :, k * D : (k + 1) * D] for k in range(FF // D)] + [w_output[layer]]
        part_a = jnp.concatenate(lines_a + [flat_rows(w_keyval)])
        part_b = jnp.concatenate(lines_b + [small_rows])
    masks = jnp.arange(half, dtype=jnp.int32)
    places = jnp.stack([upper * half + (masks ^ replica), (1 - upper) * half + (masks ^ replica)]).astype(jnp.int32)
    order = places.reshape(-1)
    inverse = jnp.zeros((replicas,), jnp.int32).at[order].set(jnp.arange(replicas, dtype=jnp.int32))
    tail_rows = part_a.shape[0] - 2 * body_rows
    flag = native.astype(jnp.int32).reshape(1)


    def use_tails(own_tails, other_tails):
        own_tails, other_tails = jnp.stack(own_tails), jnp.stack(other_tails)
        in_order = lambda picked: jnp.take(picked, inverse, axis=0)
        kv_all = in_order(jnp.where(native, own_tails, other_tails))
        small_all = in_order(jnp.where(native, other_tails, own_tails))
        if kernels:
            kv_weight = kv_all.reshape(replicas, 16, width // 16, LANES).swapaxes(1, 2).reshape(D, LANES)
        else:
            kv_weight = kv_all.reshape(replicas, -1)[:, : w_keyval.size].reshape(D, LANES)
        cuts = []
        used = 0
        for shape, count in zip(small_shapes, small_counts):
            size = math.prod(shape) // count
            cuts.append(small_all[:, used : used + count, :size].reshape((replicas,) + shape))
            used += count
        gains, shifts, biases = (
            jnp.moveaxis(cut, 0, 2).reshape(cut.shape[1:3] + (D,)).astype(F32) for cut in cuts[:3]
        )
        kv_bias = cuts[3].reshape(LANES).astype(F32)
        up_rows = jnp.moveaxis(cuts[4], 0, 1).reshape(2, FF // D, D).astype(F32)
        kv_row = jnp.zeros((2, 1, D), F32).at[0, 0, :LANES].set(kv_bias)
        params = jnp.concatenate(
            [
                gains,
                shifts,
                biases[:, 0:1],
                biases[:, 1:2] + biases[:, 2:3],
                up_rows,
                kv_row,
                jnp.zeros((2, PRM_ROWS - 7 - FF // D, D), F32),
            ],
            axis=1,
        )
        return params, kv_weight

    late = lambda done: whole_rows(*after([inputs, out_cotangent], done))
    own, other, (params, kv_weight), (fresh, given) = spread(
        part_a, part_b, native, half, tail_rows, [other_positions], [tables], use_tails, late
    )
    in_order = lambda picked: jnp.take(picked, inverse, axis=0)
    if kernels:
        weights = resident(jnp.concatenate([flag, order]), own, other, width, wide)
    else:
        mine, theirs = jnp.stack(own[0] + own[1]), jnp.stack(other[0] + other[1])
        all_a, all_b = in_order(jnp.where(native, mine, theirs)), in_order(jnp.where(native, theirs, mine))
        by_layer = lambda item: item[:, : 2 * body_rows].reshape(replicas, 2, body_rows, D).swapaxes(0, 1)
        all_a, all_b = by_layer(all_a), by_layer(all_b)
        up_part = jnp.swapaxes(all_b[:, :, :wide].reshape(2, replicas, FF // D, width, D), 2, 3)
        sources = [
            all_a[:, :, wide:].reshape(2, D, D),
            all_b[:, :, wide:].reshape(2, D, D),
            up_part.reshape(2, D, FF),
            all_a[:, :, :wide].reshape(2, FF, D),
        ]
        weights = resident(None, sources, [], width, wide)

    fixed = (params, tables, kv_weight)
    blank = jnp.zeros((rows, D), BF16)
    scalars = stage.astype(jnp.int32).reshape(1)

    slots = lambda shape, dtype=BF16: jax.ShapeDtypeStruct((micro_count,) + shape, dtype)
    per_layer = [
        *[slots((rows, D)) for _ in range(5)],
        slots((rows, FF)),
        slots((rows, FF)),
        slots((PAIRS * rows, 2 * LANES)),
        slots((rows, LANES), F32),
    ]
    stash = per_layer + per_layer + [slots((rows, LANES))]
    ticks = micro_count + 2 * (stage_count - 1)

    leaving, incoming, finals = blank, blank, slots((rows, D))
    for tick in range(ticks):
        arriving = send(leaving, to_stage(1, stage_count)) if 0 < tick < ticks - 1 else blank
        leaving, finals, stash = forward_tick(
            tick, scalars, fixed, fresh, incoming, weights, finals, stash, rows
        )
        incoming = arriving
    names = {name: (stash[k], stash[9 + k]) for k, name in enumerate(FWD_STASH)}
    back_stash = [names[name][layer] for layer in range(2) for name in ("q", "n", "w", "p", "r")] + [stash[18]]
    outs = []
    for layer in range(2):
        outs += [slots((rows, D)), slots((rows, FF)), slots((rows, D))]
    outs += [slots((rows, LANES)), slots((2, PRM_ROWS, D), F32)]

    leaving, incoming, starts = blank, blank, slots((rows, D))
    for tick in range(ticks):
        arriving = send(leaving, to_stage(-1, stage_count)) if 0 < tick < ticks - 1 else blank
        leaving, starts, outs = backward_tick(
            tick, stage_count, scalars, fixed, given, incoming, weights, back_stash, starts, outs, rows
        )
        incoming = arriving
    final, input_grad = home_rows(finals, starts)

    flat = lambda item: item.reshape(-1, item.shape[-1])
    sums = jnp.sum(outs[7], axis=0)
    by_shard = lambda item: jnp.moveaxis(item.reshape(item.shape[:2] + (replicas, -1)), 2, 0)
    up_sums = by_shard(sums[:, 6 : 6 + FF // D].reshape(2, 1, FF))
    tail = [
        by_shard(sums[:, 0:2]),
        by_shard(sums[:, 2:4]),
        by_shard(jnp.stack([sums[:, 4], sums[:, 5], sums[:, 5]], axis=1)),
        sums[0, 10, :LANES].reshape(replicas, -1),
        up_sums,
    ]
    tail = [item.reshape(replicas, count, -1) for item, count in zip(tail, small_counts)]
    tail = jnp.concatenate([jnp.pad(item, ((0, 0), (0, 0), (0, D - item.shape[2]))) for item in tail], axis=1)
    tail = tail.astype(BF16)

    def make_parts(layer, done):
        (d_low, u_low, q_low), (a_low, m_low, o_low, g_low) = (
            outs[3 * layer : 3 * layer + 3],
            [names[name][layer] for name in "amog"],
        )
        inputs = [flat(item) for item in (g_low, d_low, u_low, m_low, a_low, q_low, o_low)]
        inputs = after(inputs, done) if done else inputs
        g_low, d_low, u_low, m_low, a_low, q_low, o_low = inputs
        if kernels:
            lead = jnp.concatenate([native.astype(jnp.int32).reshape(1), order])
            more = [flat(outs[6]), tail] if layer == 0 else []
            kept, given = weight_grads(lead, inputs, more, layer, replicas)
            return [kept[:half], kept[half:]], [given[:half], given[half:]]
        product = lambda left, right: tn(left, right).astype(BF16)
        part_a = [
            product(g_low, d_low).reshape(replicas, wide, D),
            product(a_low, q_low).reshape(replicas, width, D),
        ]
        up = product(m_low, u_low).reshape(replicas, width, FF // D, D)
        part_b = [
            jnp.moveaxis(up, 2, 1).reshape(replicas, wide, D),
            product(o_low, d_low).reshape(replicas, width, D),
        ]
        if layer == 0:
            kv_grad = product(a_low, flat(outs[6])).reshape(replicas, -1)
            part_a.append(pad_rows(kv_grad, 16 * D).reshape(replicas, -1, D))
            part_b.append(tail)
        both = jnp.stack([jnp.concatenate(part_a, axis=1), jnp.concatenate(part_b, axis=1)])

        def pick(which):
            return [
                [
                    lax.dynamic_slice(both, (which, places[kind, mask], 0, 0), (1, 1) + both.shape[2:])[0, 0]
                    for mask in range(half)
                ]
                for kind in range(2)
            ]

        mine = jnp.where(native, 0, 1)
        return pick(mine), pick(1 - mine)

    shares = reduce_home(make_parts, native, half, [final, input_grad])
    grad_down = jnp.stack([part_a[:wide] for part_a, part_b in shares]).astype(F32)
    grad_query = jnp.stack([part_a[wide:body_rows] for part_a, part_b in shares]).astype(F32)
    grad_up = jnp.stack(
        [jnp.moveaxis(part_b[:wide].reshape(FF // D, width, D), 0, 1).reshape(width, FF) for part_a, part_b in shares]
    ).astype(F32)
    grad_output = jnp.stack([part_b[wide:body_rows] for part_a, part_b in shares]).astype(F32)
    kv_rows = shares[0][0][body_rows:]
    if kernels:
        kv_rows = kv_rows.reshape(16, width // 16, LANES).swapaxes(0, 1)
    grad_keyval = kv_rows.reshape(-1)[: w_keyval.size].reshape(w_keyval.shape).astype(F32)
    tail = shares[0][1][body_rows:].astype(F32)
    small = []
    used = 0
    for shape, count in zip(small_shapes, small_counts):
        small.append(tail[used : used + count, : math.prod(shape) // count].reshape(shape))
        used += count
    return (
        final,
        input_grad,
        small[0],
        small[1],
        small[2],
        grad_query,
        grad_keyval,
        small[3],
        grad_output,
        grad_up,
        small[4],
        grad_down,
    )


def solution(mesh):
    return jax.shard_map(
        body,
        mesh=mesh,
        in_specs=(
            P("dp", "pipe", None),
            P("dp", "pipe", None),
            P("dp", None),
            P("pipe", None, "dp"),
            P("pipe", None, "dp"),
            P("pipe", None, "dp"),
            P("pipe", "dp", None),
            P("pipe", "dp", None),
            P("pipe", "dp"),
            P("pipe", "dp", None),
            P("pipe", "dp", None),
            P("pipe", "dp"),
            P("pipe", "dp", None),
        ),
        out_specs=(
            P("dp", "pipe", None),
            P("dp", "pipe", None),
            P("pipe", None, "dp"),
            P("pipe", None, "dp"),
            P("pipe", None, "dp"),
            P("pipe", "dp", None),
            P("pipe", "dp", None),
            P("pipe", "dp"),
            P("pipe", "dp", None),
            P("pipe", "dp", None),
            P("pipe", "dp"),
            P("pipe", "dp", None),
        ),
        check_vma=False,
    )
```

time: 2570 us -> 661 us (0.26)
  waiting for transfers between devices: 1440 us -> 313 us
  matrix products: 314 us -> 0 us
  other arithmetic: 295 us -> 21.7 us
  blocking collectives: 198 us -> 0 us
  Pallas kernels: 0 us -> 186 us
  local copies, waits for them, and re-layouts: 147 us -> 33.4 us
  loops' own time: 31.6 us -> 0 us
    reduce_scatter x7 -> x0, waiting for transfers between devices: 581 us -> none  [the longest x1 165 us: body(): lax.psum_scatter(sums[7].astype(jnp.bfloat16), 'dp', scatter_dimension=1,...]
    dot_general x192 -> x0, matrix products: 314 us -> none  [the longest x12 68.3 us: layer_forward(): jnp.dot(act_low, w_down[sublayer], preferred_element_type=jnp.float32)]
    unnamed x21 -> x0, waiting for transfers between devices: 264 us -> none
    all_gather x4 -> x0, waiting for transfers between devices: 191 us -> none  [the longest x1 138 us: body(): lax.all_gather(shards[9], 'dp', axis=1, tiled=True)]
    pallas_call x0 -> x24, Pallas kernels: none -> 186 us  [the longest x20 144 us: call_tick(): pl.pallas_call(kernel, out_shape=shapes, in_specs=[pl.BlockSpec(memory_sp...]
    all_gather x7 -> x0, blocking collectives: 176 us -> none  [the longest x1 33.6 us: body(): lax.all_gather(shards[4], 'dp', axis=1, tiled=True)]
    add x68 -> x2, other arithmetic: 144 us -> 0.02 us  [the longest x1 0.01 us: use_tails(): biases[:, 1:2] + biases[:, 2:3]]
    ppermute x14 -> x79, waiting for transfers between devices: 399 us -> 313 us  [send(): return lax.ppermute(value, ('dp', 'pipe'), pairs)]
  transfers between devices with their start and end apart: 30 -> 79, of which waited for: 21 -> 33; matrix products, arithmetic and copies ran while one was open for 3% -> 6% of each run, Pallas kernels for 0% -> 21%
where the time goes in v1:
time: 661 us; the launch traced here: 650 us
  waiting for transfers between devices  313 us (47%)
  Pallas kernels  186 us (28%)
  starting transfers between devices  93.4 us (14%)
  local copies, waits for them, and re-layouts  33.4 us (5%)
  other arithmetic  21.7 us (3%)
    ppermute x79, waiting for transfers between devices, send(): return lax.ppermute(value, ('dp', 'pipe'), pairs)  313 us
    pallas_call x20, Pallas kernels, call_tick(): pl.pallas_call(kernel, out_shape=shapes, in_specs=[pl.BlockSpec(memory_sp...  144 us
    ppermute x79, starting transfers between devices, send(): return lax.ppermute(value, ('dp', 'pipe'), pairs)  93.4 us
    pallas_call x2, Pallas kernels, weight_grads(): pl.pallas_call(lambda *refs: weight_grad_kernel(layer, count, *refs), out...  30.3 us
  transfers between devices with their start and end apart: 79, of which 33 were waited for; matrix products, arithmetic and copies ran while one was open for 6% of the time, Pallas kernels for 21%

profile of v1, /device:TPU:0, one launch (start us, length us, event | category | flops | bytes accessed | tf_op | source)
XLA Modules:
  0.0 650.4 jit_solution(12502805531470029985)
XLA Ops:
  1.9 3.9 pack_shard.1
  6.3 3.7 collective-permute-start.1
  10.0 2.7 broadcast_select_fusion
  12.7 3.4 collective-permute-start.2
  17.6 1.6 collective-permute-start.4
  22.6 59.1 %collective-permute-done.2.refs_6_ = bf16[976,768]{1,0:T(8,128)(2,1)} collective-permute-done((bf16[976,768]{1,0:T(8,128)(2,1)}, bf16[976,768]{1,0:T(8,128)(2,1)}, u32[]{:S(2)}, u32[]{:S(2)}) %collective-permute-start.2) | collective-permute-done | bytes 1499168 | tf_op jit(solution)/shard_map/ppermute | solution.py:55
  91.7 15.2 %collective-permute-done.11 = bf16[16,768]{1,0:T(8,128)(2,1)S(1)} collective-permute-done((bf16[16,768]{1,0:T(8,128)(2,1)S(1)}, bf16[16,768]{1,0:T(8,128)(2,1)S(1)}, u32[]{:S(2)}, u32[]{:S(2)}) %collective-permute-start.11) | collective-permute-done | bytes 24608 | tf_op jit(solution)/shard_map/ppermute | solution.py:55
  109.8 24.4 %collective-permute-done.6.refs_7_ = bf16[976,768]{1,0:T(8,128)(2,1)} collective-permute-done((bf16[976,768]{1,0:T(8,128)(2,1)}, bf16[976,768]{1,0:T(8,128)(2,1)}, u32[]{:S(2)}, u32[]{:S(2)}) %collective-permute-start.6) | collective-permute-done | bytes 1499168 | tf_op jit(solution)/shard_map/ppermute | solution.py:55
  134.3 1.7 collective-permute-done.7.refs_8_
  139.5 2.0 slice.219
  141.5 2.0 slice.220
  144.1 1.7 collective-permute-start.22
  149.4 1.6 gather_fusion.1
  158.9 3.9 collective-permute-done.22.refs_9_
  162.8 3.4 collective-permute-done.23.refs_10_
  166.8 3.4 collective-permute-start.20
  171.6 2.9 collective-permute-done.20
  174.5 2.7 collective-permute-done.21
  179.2 8.3 %gather_shards.1 = (bf16[2,768,768]{2,1,0:T(8,128)(2,1)S(1)}, bf16[2,768,768]{2,1,0:T(8,128)(2,1)S(1)}, bf16[2,768,3072]{2,1,0:T(8,128)(2,1)S(1)}, bf16[2,3072,768]{2,1,0:T(8,128)(2,1)S(1)}) custom-call(s32[9]{0:T(128)S(1)} %pad_add_fusion.1.refs_0_, bf16[976,768]{1,0:T(8,128)(2,1)} %copy-done.5, bf16[976,768]{1,0:T(8,128)(2,1)} %collective-permute-done.3.refs_2_, ...), custom_call_target="tpu_custom_call" | custom-call | tf_op jit(solution)/shard_map/gather_shards/pallas_call | solution.py:239
  187.5 12.4 %forward_tick.10 = (bf16[128,768]{1,0:T(8,128)(2,1)S(1)}, bf16[4,128,768]{2,1,0:T(8,128)(2,1)}, bf16[4,128,768]{2,1,0:T(8,128)(2,1)}, bf16[4,128,768]{2,1,0:T(8,...) custom-call(s32[1]{0:T(128)} %bitcast.refs_0_, ...), custom_call_target="tpu_custom_call" | custom-call | flops 3019898880 | bytes 10000000 | tf_op jit(solution)/shard_map/forward_tick/pallas_call | solution.py:655
  201.2 13.2 %forward_tick.11 = (bf16[128,768]{1,0:T(8,128)(2,1)S(1)}, bf16[4,128,768]{2,1,0:T(8,128)(2,1)}, bf16[4,128,768]{2,1,0:T(8,128)(2,1)}, bf16[4,128,768]{2,1,0:T(8,...) custom-call(s32[1]{0:T(128)} %bitcast.refs_0_, ...), custom_call_target="tpu_custom_call", output_to_operand_aliasing={{1}: (10, {}), {2}: (11, {}), {3}: (12, {}), {4}: (13, {}),... | custom-call | flops 3019898880 | bytes 10000000 | tf_op jit(solution)/shard_map/forward_tick/pallas_call | solution.py:655
  215.8 12.4 %forward_tick.12 = (bf16[128,768]{1,0:T(8,128)(2,1)S(1)}, bf16[4,128,768]{2,1,0:T(8,128)(2,1)}, bf16[4,128,768]{2,1,0:T(8,128)(2,1)}, bf16[4,128,768]{2,1,0:T(8,...) custom-call(s32[1]{0:T(128)} %bitcast.refs_0_, ...), custom_call_target="tpu_custom_call", output_to_operand_aliasing={{1}: (10, {}), {2}: (11, {}), {3}: (12, {}), {4}: (13, {}),... | custom-call | flops 3019898880 | bytes 10000000 | tf_op jit(solution)/shard_map/forward_tick/pallas_call | solution.py:655
  229.6 12.4 %forward_tick.13 = (bf16[128,768]{1,0:T(8,128)(2,1)S(1)}, bf16[4,128,768]{2,1,0:T(8,128)(2,1)}, bf16[4,128,768]{2,1,0:T(8,128)(2,1)}, bf16[4,128,768]{2,1,0:T(8,...) custom-call(s32[1]{0:T(128)} %bitcast.refs_0_, ...), custom_call_target="tpu_custom_call", output_to_operand_aliasing={{1}: (10, {}), {2}: (11, {}), {3}: (12, {}), {4}: (13, {}),... | custom-call | flops 3019898880 | bytes 10000000 | tf_op jit(solution)/shard_map/forward_tick/pallas_call | solution.py:655
  243.3 6.8 %forward_tick.14 = (bf16[128,768]{1,0:T(8,128)(2,1)S(1)}, bf16[4,128,768]{2,1,0:T(8,128)(2,1)}, bf16[4,128,768]{2,1,0:T(8,128)(2,1)}, bf16[4,128,768]{2,1,0:T(8,...) custom-call(s32[1]{0:T(128)} %bitcast.refs_0_, ...), custom_call_target="tpu_custom_call", output_to_operand_aliasing={{1}: (10, {}), {2}: (11, {}), {3}: (12, {}), {4}: (13, {}),... | custom-call | flops 3019898880 | bytes 10000000 | tf_op jit(solution)/shard_map/forward_tick/pallas_call | solution.py:655
  250.1 1.8 collective-permute-start.32
  252.3 14.3 %collective-permute-start.31 = (bf16[128,768]{1,0:T(8,128)(2,1)S(1)}, bf16[128,768]{1,0:T(8,128)(2,1)S(1)}, u32[]{:S(2)}, u32[]{:S(2)}) collective-permute-start(bf16[128,768]{1,0:T(8,128)(2,1)S(1)} %get-tuple-element.530), channel_id=1, source_target_pairs={{0,16},{1,17},{4,20},{5,21},{8,24},{9,25},{12,28},{13,29},{16,18},... | collective-permute-start | bytes 589832 | tf_op jit(solution)/shard_map/ppermute | solution.py:55
  266.9 1.9 collective-permute-start.34
  269.7 6.7 %forward_tick.17 = (bf16[128,768]{1,0:T(8,128)(2,1)S(1)}, bf16[4,128,768]{2,1,0:T(8,128)(2,1)}, bf16[4,128,768]{2,1,0:T(8,128)(2,1)}, bf16[4,128,768]{2,1,0:T(8,...) custom-call(s32[1]{0:T(128)} %bitcast.refs_0_, ...), custom_call_target="tpu_custom_call", output_to_operand_aliasing={{1}: (10, {}), {2}: (11, {}), {3}: (12, {}), {4}: (13, {}),... | custom-call | flops 3019898880 | bytes 10000000 | tf_op jit(solution)/shard_map/forward_tick/pallas_call | solution.py:655
  276.4 5.3 collective-permute-start.33
  282.0 2.9 collective-permute-done.33.refs_5_
  285.2 7.1 %backward_tick.10 = (bf16[128,768]{1,0:T(8,128)(2,1)S(1)}, bf16[4,128,768]{2,1,0:T(8,128)(2,1)}, bf16[4,128,768]{2,1,0:T(8,128)(2,1)}, bf16[4,128,3072]{2,1,0:T(...) custom-call(s32[1]{0:T(128)} %bitcast.refs_0_, ...), custom_call_target="tpu_custom_call" | custom-call | flops 3019898880 | bytes 10000000 | tf_op jit(solution)/shard_map/backward_tick/pallas_call | solution.py:655
  295.2 9.2 %collective-permute-done.36.refs_5_ = bf16[128,768]{1,0:T(8,128)(2,1)S(1)} collective-permute-done((bf16[128,768]{1,0:T(8,128)(2,1)S(1)}, bf16[128,768]{1,0:T(8,128)(2,1)S(1)}, u32[]{:S(2)}, u32[]{:S(2)}) %collective-permute-start.36) | collective-permute-done | bytes 196640 | tf_op jit(solution)/shard_map/ppermute | solution.py:55
  305.9 2.7 collective-permute-done.35.refs_5_
  308.6 6.8 %backward_tick.13 = (bf16[128,768]{1,0:T(8,128)(2,1)S(1)}, bf16[4,128,768]{2,1,0:T(8,128)(2,1)}, bf16[4,128,768]{2,1,0:T(8,128)(2,1)}, bf16[4,128,3072]{2,1,0:T(...) custom-call(s32[1]{0:T(128)} %bitcast.refs_0_, ...), custom_call_target="tpu_custom_call", output_to_operand_aliasing={{1}: (21, {}), {2}: (22, {}), {3}: (23, {}), {4}: (24, {}),... | custom-call | flops 3019898880 | bytes 10000000 | tf_op jit(solution)/shard_map/backward_tick/pallas_call | solution.py:655
  316.8 10.2 %collective-permute-done.38.refs_5_ = bf16[128,768]{1,0:T(8,128)(2,1)S(1)} collective-permute-done((bf16[128,768]{1,0:T(8,128)(2,1)S(1)}, bf16[128,768]{1,0:T(8,128)(2,1)S(1)}, u32[]{:S(2)}, u32[]{:S(2)}) %collective-permute-start.38) | collective-permute-done | bytes 196640 | tf_op jit(solution)/shard_map/ppermute | solution.py:55
  328.4 6.9 %collective-permute-done.37.refs_5_ = bf16[128,768]{1,0:T(8,128)(2,1)S(1)} collective-permute-done((bf16[128,768]{1,0:T(8,128)(2,1)S(1)}, bf16[128,768]{1,0:T(8,128)(2,1)S(1)}, u32[]{:S(2)}, u32[]{:S(2)}) %collective-permute-start.37) | collective-permute-done | bytes 196640 | tf_op jit(solution)/shard_map/ppermute | solution.py:55
  336.9 39.8 %collective-permute-done.40.refs_5_ = bf16[128,768]{1,0:T(8,128)(2,1)S(1)} collective-permute-done((bf16[128,768]{1,0:T(8,128)(2,1)S(1)}, bf16[128,768]{1,0:T(8,128)(2,1)S(1)}, u32[]{:S(2)}, u32[]{:S(2)}) %collective-permute-start.40) | collective-permute-done | bytes 196640 | tf_op jit(solution)/shard_map/ppermute | solution.py:55
  376.7 16.6 %backward_tick.16 = (bf16[128,768]{1,0:T(8,128)(2,1)S(1)}, bf16[4,128,768]{2,1,0:T(8,128)(2,1)}, bf16[4,128,768]{2,1,0:T(8,128)(2,1)}, bf16[4,128,3072]{2,1,0:T(...) custom-call(s32[1]{0:T(128)} %bitcast.refs_0_, ...), custom_call_target="tpu_custom_call", output_to_operand_aliasing={{1}: (21, {}), {2}: (22, {}), {3}: (23, {}), {4}: (24, {}),... | custom-call | flops 3019898880 | bytes 10000000 | tf_op jit(solution)/shard_map/backward_tick/pallas_call | solution.py:655
  394.9 15.8 %backward_tick.17 = (bf16[128,768]{1,0:T(8,128)(2,1)S(1)}, bf16[4,128,768]{2,1,0:T(8,128)(2,1)}, bf16[4,128,768]{2,1,0:T(8,128)(2,1)}, bf16[4,128,3072]{2,1,0:T(...) custom-call(s32[1]{0:T(128)} %bitcast.refs_0_, ...), custom_call_target="tpu_custom_call", output_to_operand_aliasing={{1}: (21, {}), {2}: (22, {}), {3}: (23, {}), {4}: (24, {}),... | custom-call | flops 3019898880 | bytes 10000000 | tf_op jit(solution)/shard_map/backward_tick/pallas_call | solution.py:655
  413.5 15.5 %backward_tick.18 = (bf16[128,768]{1,0:T(8,128)(2,1)}, bf16[4,128,768]{2,1,0:T(8,128)(2,1)}, bf16[4,128,768]{2,1,0:T(8,128)(2,1)}, bf16[4,128,3072]{2,1,0:T(8,12...) custom-call(s32[1]{0:T(128)} %bitcast.refs_0_, ...), custom_call_target="tpu_custom_call", output_to_operand_aliasing={{1}: (21, {}), {2}: (22, {}), {3}: (23, {}), {4}: (24, {}),... | custom-call | flops 3019898880 | bytes 10000000 | tf_op jit(solution)/shard_map/backward_tick/pallas_call | solution.py:655
  429.0 2.3 collective-permute-done.41.refs_5_
  431.3 15.9 %backward_tick.19 = (bf16[128,768]{1,0:T(8,128)(2,1)}, bf16[4,128,768]{2,1,0:T(8,128)(2,1)}, bf16[4,128,768]{2,1,0:T(8,128)(2,1)}, bf16[4,128,3072]{2,1,0:T(8,12...) custom-call(s32[1]{0:T(128)} %bitcast.refs_0_, ...), custom_call_target="tpu_custom_call", output_to_operand_aliasing={{1}: (21, {}), {2}: (22, {}), {3}: (23, {}), {4}: (24, {}),... | custom-call | flops 3019898880 | bytes 10000000 | tf_op jit(solution)/shard_map/backward_tick/pallas_call | solution.py:655
  453.2 4.8 collective-permute-start.46
  458.0 14.4 %weight_grads.2 = (bf16[480,768]{1,0:T(8,128)(2,1)}, bf16[480,768]{1,0:T(8,128)(2,1)}, bf16[480,768]{1,0:T(8,128)(2,1)}, bf16[480,768]{1,0:T(8,128)(2,1)}, bf16[...) custom-call(s32[9]{0:T(128)} %copy-done.1, ...), custom_call_target="tpu_custom_call" | custom-call | flops 6039797760 | bytes 22000000 | tf_op jit(solution)/shard_map/weight_grads/pallas_call | solution.py:314
  475.9 15.9 %weight_grads.3 = (bf16[496,768]{1,0:T(8,128)(2,1)}, bf16[496,768]{1,0:T(8,128)(2,1)}, bf16[496,768]{1,0:T(8,128)(2,1)}, bf16[496,768]{1,0:T(8,128)(2,1)}, bf16[...) custom-call(s32[9]{0:T(128)} %copy-done.1, ...), custom_call_target="tpu_custom_call" | custom-call | flops 6039797760 | bytes 22000000 | tf_op jit(solution)/shard_map/weight_grads/pallas_call | solution.py:314
  494.5 2.1 collective-permute-start.52
  498.5 1.6 collective-permute-start.49
  501.5 12.4 %collective-permute-done.52 = bf16[480,768]{1,0:T(8,128)(2,1)S(1)} collective-permute-done((bf16[480,768]{1,0:T(8,128)(2,1)S(1)}, bf16[480,768]{1,0:T(8,128)(2,1)S(1)}, u32[]{:S(2)}, u32[]{:S(2)}) %collective-permute-start.52) | collective-permute-done | bytes 737312 | tf_op jit(solution)/shard_map/ppermute | solution.py:55
  514.2 2.6 collective-permute-done.55
  517.2 12.0 %collective-permute-done.49 = bf16[480,768]{1,0:T(8,128)(2,1)S(1)} collective-permute-done((bf16[480,768]{1,0:T(8,128)(2,1)S(1)}, bf16[480,768]{1,0:T(8,128)(2,1)S(1)}, u32[]{:S(2)}, u32[]{:S(2)}) %collective-permute-start.49) | collective-permute-done | bytes 737312 | tf_op jit(solution)/shard_map/ppermute | solution.py:55
  529.2 2.9 collective-permute-done.57
  533.8 1.6 collective-permute-start.60
  536.0 15.0 %collective-permute-done.58 = bf16[480,768]{1,0:T(8,128)(2,1)S(1)} collective-permute-done((bf16[480,768]{1,0:T(8,128)(2,1)S(1)}, bf16[480,768]{1,0:T(8,128)(2,1)S(1)}, u32[]{:S(2)}, u32[]{:S(2)}) %collective-permute-start.58) | collective-permute-done | bytes 737312 | tf_op jit(solution)/shard_map/ppermute | solution.py:55
  551.4 1.6 collective-permute-done.60
  553.5 1.6 collective-permute-start.75
  555.9 17.1 %collective-permute-done.75 = bf16[480,768]{1,0:T(8,128)(2,1)S(1)} collective-permute-done((bf16[480,768]{1,0:T(8,128)(2,1)S(1)}, bf16[480,768]{1,0:T(8,128)(2,1)S(1)}, u32[]{:S(2)}, u32[]{:S(2)}) %collective-permute-start.75) | collective-permute-done | bytes 737312 | tf_op jit(solution)/shard_map/ppermute | solution.py:55
  572.9 1.5 collective-permute-start.73
  576.0 13.2 %collective-permute-done.69 = bf16[496,768]{1,0:T(8,128)(2,1)S(1)} collective-permute-done((bf16[496,768]{1,0:T(8,128)(2,1)S(1)}, bf16[496,768]{1,0:T(8,128)(2,1)S(1)}, u32[]{:S(2)}, u32[]{:S(2)}) %collective-permute-start.69) | collective-permute-done | bytes 761888 | tf_op jit(solution)/shard_map/ppermute | solution.py:55
  589.7 1.7 collective-permute-done.77
  592.8 12.3 %collective-permute-done.73 = bf16[480,768]{1,0:T(8,128)(2,1)S(1)} collective-permute-done((bf16[480,768]{1,0:T(8,128)(2,1)S(1)}, bf16[480,768]{1,0:T(8,128)(2,1)S(1)}, u32[]{:S(2)}, u32[]{:S(2)}) %collective-permute-start.73) | collective-permute-done | bytes 737312 | tf_op jit(solution)/shard_map/ppermute | solution.py:55
  607.8 18.6 %collective-permute-done.65 = bf16[496,768]{1,0:T(8,128)(2,1)S(1)} collective-permute-done((bf16[496,768]{1,0:T(8,128)(2,1)S(1)}, bf16[496,768]{1,0:T(8,128)(2,1)S(1)}, u32[]{:S(2)}, u32[]{:S(2)}) %collective-permute-start.65) | collective-permute-done | bytes 761888 | tf_op jit(solution)/shard_map/ppermute | solution.py:55
  626.4 11.1 %collective-permute-done.70 = bf16[496,768]{1,0:T(8,128)(2,1)S(1)} collective-permute-done((bf16[496,768]{1,0:T(8,128)(2,1)S(1)}, bf16[496,768]{1,0:T(8,128)(2,1)S(1)}, u32[]{:S(2)}, u32[]{:S(2)}) %collective-permute-start.70) | collective-permute-done | bytes 761888 | tf_op jit(solution)/shard_map/ppermute | solution.py:55
  639.8 1.6 maximum_convert_fusion.1
  648.4 1.6 maximum_convert_fusion
  (342 shorter events, 94.0 us)
Async XLA Ops:
  12.7 69.1 %collective-permute-start.2 = (bf16[976,768]{1,0:T(8,128)(2,1)}, bf16[976,768]{1,0:T(8,128)(2,1)}, u32[]{:S(2)}, u32[]{:S(2)}) collective-permute-start(bf16[976,768]{1,0:T(8,128)(2,1)} %get-tuple-element.404), channel_id=1, source_target_pairs={{0,16},{1,17},{2,18},{3,19},{4,20},{5,21},{6,22},{7,23},{8,24},{9,... | collective-permute-start | bytes 4497416 | tf_op jit(solution)/shard_map/ppermute | solution.py:55
  16.1 65.7 %collective-permute-start.3 = (bf16[976,768]{1,0:T(8,128)(2,1)S(1)}, bf16[976,768]{1,0:T(8,128)(2,1)}, u32[]{:S(2)}, u32[]{:S(2)}) collective-permute-start(bf16[976,768]{1,0:T(8,128)(2,1)S(1)} %get-tuple-element.405.refs_1_), channel_id=1, source_target_pairs={{0,4},{1,5},{2,6},{3,7},{4,0},{5,1},{6,2},{7,3},{8,12},{9,13},{10,... | collective-permute-start | bytes 4497416 | tf_op jit(solution)/shard_map/ppermute | solution.py:55
  17.6 65.4 %collective-permute-start.4 = (bf16[976,768]{1,0:T(8,128)(2,1)S(1)}, bf16[976,768]{1,0:T(8,128)(2,1)}, u32[]{:S(2)}, u32[]{:S(2)}) collective-permute-start(bf16[976,768]{1,0:T(8,128)(2,1)S(1)} %get-tuple-element.405.refs_1_), channel_id=1, source_target_pairs={{0,8},{1,9},{2,10},{3,11},{4,12},{5,13},{6,14},{7,15},{8,0},{9,1},... | collective-permute-start | bytes 4497416 | tf_op jit(solution)/shard_map/ppermute | solution.py:55
  19.2 63.8 %collective-permute-start.5 = (bf16[976,768]{1,0:T(8,128)(2,1)S(1)}, bf16[976,768]{1,0:T(8,128)(2,1)}, u32[]{:S(2)}, u32[]{:S(2)}) collective-permute-start(bf16[976,768]{1,0:T(8,128)(2,1)S(1)} %get-tuple-element.405.refs_1_), channel_id=1, source_target_pairs={{0,1},{1,0},{2,3},{3,2},{4,5},{5,4},{6,7},{7,6},{8,9},{9,8},{10,11... | collective-permute-start | bytes 4497416 | tf_op jit(solution)/shard_map/ppermute | solution.py:55
  84.2 23.2 %collective-permute-start.13 = (bf16[496,768]{1,0:T(8,128)(2,1)S(1)}, bf16[496,768]{1,0:T(8,128)(2,1)}, u32[]{:S(2)}, u32[]{:S(2)}) collective-permute-start(bf16[496,768]{1,0:T(8,128)(2,1)S(1)} %slice.198), channel_id=1, source_target_pairs={{0,4},{1,5},{2,6},{3,7},{4,0},{5,1},{6,2},{7,3},{8,12},{9,13},{10,... | collective-permute-start | bytes 2285576 | tf_op jit(solution)/shard_map/ppermute | solution.py:55
  86.0 20.9 %collective-permute-start.12 = (bf16[480,768]{1,0:T(8,128)(2,1)S(1)}, bf16[480,768]{1,0:T(8,128)(2,1)}, u32[]{:S(2)}, u32[]{:S(2)}) collective-permute-start(bf16[480,768]{1,0:T(8,128)(2,1)S(1)} %slice.197), channel_id=1, source_target_pairs={{0,8},{1,9},{2,10},{3,11},{4,12},{5,13},{6,14},{7,15},{8,0},{9,1},... | collective-permute-start | bytes 2211848 | tf_op jit(solution)/shard_map/ppermute | solution.py:55
  88.2 18.7 %collective-permute-start.11 = (bf16[16,768]{1,0:T(8,128)(2,1)S(1)}, bf16[16,768]{1,0:T(8,128)(2,1)S(1)}, u32[]{:S(2)}, u32[]{:S(2)}) collective-permute-start(bf16[16,768]{1,0:T(8,128)(2,1)S(1)} %slice.196), channel_id=1, source_target_pairs={{0,12},{1,13},{2,14},{3,15},{4,8},{5,9},{6,10},{7,11},{8,4},{9,5},... | collective-permute-start | bytes 73736 | tf_op jit(solution)/shard_map/ppermute | solution.py:55
  89.7 44.6 %collective-permute-start.6 = (bf16[976,768]{1,0:T(8,128)(2,1)}, bf16[976,768]{1,0:T(8,128)(2,1)}, u32[]{:S(2)}, u32[]{:S(2)}) collective-permute-start(bf16[976,768]{1,0:T(8,128)(2,1)} %collective-permute-done.2.refs_6_), channel_id=1, source_target_pairs={{0,4},{1,5},{2,6},{3,7},{4,0},{5,1},{6,2},{7,3},{8,12},{9,13},{10,... | collective-permute-start | bytes 4497416 | tf_op jit(solution)/shard_map/ppermute | solution.py:55
  90.3 45.7 %collective-permute-start.7 = (bf16[976,768]{1,0:T(8,128)(2,1)}, bf16[976,768]{1,0:T(8,128)(2,1)}, u32[]{:S(2)}, u32[]{:S(2)}) collective-permute-start(bf16[976,768]{1,0:T(8,128)(2,1)} %collective-permute-done.2.refs_6_), channel_id=1, source_target_pairs={{0,8},{1,9},{2,10},{3,11},{4,12},{5,13},{6,14},{7,15},{8,0},{9,1},... | collective-permute-start | bytes 4497416 | tf_op jit(solution)/shard_map/ppermute | solution.py:55
  106.9 29.1 %collective-permute-start.8 = (bf16[976,768]{1,0:T(8,128)(2,1)}, bf16[976,768]{1,0:T(8,128)(2,1)}, u32[]{:S(2)}, u32[]{:S(2)}) collective-permute-start(bf16[976,768]{1,0:T(8,128)(2,1)} %collective-permute-done.3.refs_2_), channel_id=1, source_target_pairs={{0,1},{1,0},{2,3},{3,2},{4,5},{5,4},{6,7},{7,6},{8,9},{9,8},{10,11... | collective-permute-start | bytes 4497416 | tf_op jit(solution)/shard_map/ppermute | solution.py:55
  106.9 29.1 %collective-permute-start.9 = (bf16[976,768]{1,0:T(8,128)(2,1)}, bf16[976,768]{1,0:T(8,128)(2,1)}, u32[]{:S(2)}, u32[]{:S(2)}) collective-permute-start(bf16[976,768]{1,0:T(8,128)(2,1)} %collective-permute-done.4.refs_3_), channel_id=1, source_target_pairs={{0,1},{1,0},{2,3},{3,2},{4,5},{5,4},{6,7},{7,6},{8,9},{9,8},{10,11... | collective-permute-start | bytes 4497416 | tf_op jit(solution)/shard_map/ppermute | solution.py:55
  107.4 28.6 %collective-permute-start.10 = (bf16[976,768]{1,0:T(8,128)(2,1)}, bf16[976,768]{1,0:T(8,128)(2,1)}, u32[]{:S(2)}, u32[]{:S(2)}) collective-permute-start(bf16[976,768]{1,0:T(8,128)(2,1)} %collective-permute-done.2.refs_6_), channel_id=1, source_target_pairs={{0,1},{1,0},{2,3},{3,2},{4,5},{5,4},{6,7},{7,6},{8,9},{9,8},{10,11... | collective-permute-start | bytes 4497416 | tf_op jit(solution)/shard_map/ppermute | solution.py:55
  136.0 11.3 %collective-permute-start.14 = (bf16[496,768]{1,0:T(8,128)(2,1)}, bf16[496,768]{1,0:T(8,128)(2,1)S(1)}, u32[]{:S(2)}, u32[]{:S(2)}) collective-permute-start(bf16[496,768]{1,0:T(8,128)(2,1)} %collective-permute-done.13.refs_5_), channel_id=1, source_target_pairs={{0,1},{1,0},{2,3},{3,2},{4,5},{5,4},{6,7},{7,6},{8,9},{9,8},{10,11... | collective-permute-start | bytes 2285576 | tf_op jit(solution)/shard_map/ppermute | solution.py:55
  137.5 11.0 %collective-permute-start.15 = (bf16[976,768]{1,0:T(8,128)(2,1)}, bf16[976,768]{1,0:T(8,128)(2,1)S(1)}, u32[]{:S(2)}, u32[]{:S(2)}) collective-permute-start(bf16[976,768]{1,0:T(8,128)(2,1)} %collective-permute-done.6.refs_7_), channel_id=1, source_target_pairs={{0,1},{1,0},{2,3},{3,2},{4,5},{5,4},{6,7},{7,6},{8,9},{9,8},{10,11... | collective-permute-start | bytes 4497416 | tf_op jit(solution)/shard_map/ppermute | solution.py:55
  144.1 18.7 %collective-permute-start.22 = (bf16[480,768]{1,0:T(8,128)(2,1)}, bf16[480,768]{1,0:T(8,128)(2,1)}, u32[]{:S(2)}, u32[]{:S(2)}) collective-permute-start(bf16[480,768]{1,0:T(8,128)(2,1)} %slice.219), channel_id=1, source_target_pairs={{0,8},{1,9},{2,10},{3,11},{4,12},{5,13},{6,14},{7,15},{8,0},{9,1},... | collective-permute-start | bytes 2211848 | tf_op jit(solution)/shard_map/ppermute | solution.py:55
  147.2 19.0 %collective-permute-start.23 = (bf16[496,768]{1,0:T(8,128)(2,1)}, bf16[496,768]{1,0:T(8,128)(2,1)}, u32[]{:S(2)}, u32[]{:S(2)}) collective-permute-start(bf16[496,768]{1,0:T(8,128)(2,1)} %slice.220), channel_id=1, source_target_pairs={{0,4},{1,5},{2,6},{3,7},{4,0},{5,1},{6,2},{7,3},{8,12},{9,13},{10,... | collective-permute-start | bytes 2285576 | tf_op jit(solution)/shard_map/ppermute | solution.py:55
  148.5 14.3 %collective-permute-start.24 = (bf16[480,768]{1,0:T(8,128)(2,1)}, bf16[480,768]{1,0:T(8,128)(2,1)}, u32[]{:S(2)}, u32[]{:S(2)}) collective-permute-start(bf16[480,768]{1,0:T(8,128)(2,1)} %collective-permute-done.12.refs_4_), channel_id=1, source_target_pairs={{0,1},{1,0},{2,3},{3,2},{4,5},{5,4},{6,7},{7,6},{8,9},{9,8},{10,11... | collective-permute-start | bytes 2211848 | tf_op jit(solution)/shard_map/ppermute | solution.py:55
  156.6 13.6 %collective-permute-start.18 = (bf16[4,32,768]{2,1,0:T(8,128)(2,1)S(1)}, bf16[4,32,768]{2,1,0:T(8,128)(2,1)S(1)}, u32[]{:S(2)}, u32[]{:S(2)}) collective-permute-start(bf16[4,32,768]{2,1,0:T(8,128)(2,1)S(1)} %get-tuple-element.842), channel_id=1, source_target_pairs={{0,0},{2,2},{4,4},{6,6},{8,8},{10,10},{12,12},{14,14},{16,1},{18,3... | collective-permute-start | bytes 589832 | tf_op jit(solution)/shard_map/ppermute | solution.py:55
  157.3 14.2 %collective-permute-start.19 = (bf16[4,32,768]{2,1,0:T(8,128)(2,1)S(1)}, bf16[4,32,768]{2,1,0:T(8,128)(2,1)S(1)}, u32[]{:S(2)}, u32[]{:S(2)}) collective-permute-start(bf16[4,32,768]{2,1,0:T(8,128)(2,1)S(1)} %get-tuple-element.839), channel_id=1, source_target_pairs={{1,0},{3,2},{5,4},{7,6},{9,8},{11,10},{13,12},{15,14},{17,1},{19,3... | collective-permute-start | bytes 589832 | tf_op jit(solution)/shard_map/ppermute | solution.py:55
  166.2 11.1 %collective-permute-start.25 = (bf16[480,768]{1,0:T(8,128)(2,1)}, bf16[480,768]{1,0:T(8,128)(2,1)S(1)}, u32[]{:S(2)}, u32[]{:S(2)}) collective-permute-start(bf16[480,768]{1,0:T(8,128)(2,1)} %collective-permute-done.22.refs_9_), channel_id=1, source_target_pairs={{0,1},{1,0},{2,3},{3,2},{4,5},{5,4},{6,7},{7,6},{8,9},{9,8},{10,11... | collective-permute-start | bytes 2211848 | tf_op jit(solution)/shard_map/ppermute | solution.py:55
  166.2 11.1 %collective-permute-start.26 = (bf16[496,768]{1,0:T(8,128)(2,1)}, bf16[496,768]{1,0:T(8,128)(2,1)S(1)}, u32[]{:S(2)}, u32[]{:S(2)}) collective-permute-start(bf16[496,768]{1,0:T(8,128)(2,1)} %collective-permute-done.23.refs_10_), channel_id=1, source_target_pairs={{0,1},{1,0},{2,3},{3,2},{4,5},{5,4},{6,7},{7,6},{8,9},{9,8},{10,11... | collective-permute-start | bytes 2285576 | tf_op jit(solution)/shard_map/ppermute | solution.py:55
  199.9 15.9 %collective-permute-start.28 = (bf16[128,768]{1,0:T(8,128)(2,1)S(1)}, bf16[128,768]{1,0:T(8,128)(2,1)S(1)}, u32[]{:S(2)}, u32[]{:S(2)}) collective-permute-start(bf16[128,768]{1,0:T(8,128)(2,1)S(1)} %get-tuple-element.447), channel_id=1, source_target_pairs={{0,16},{1,17},{4,20},{5,21},{8,24},{9,25},{12,28},{13,29},{16,18},... | collective-permute-start | bytes 589832 | tf_op jit(solution)/shard_map/ppermute | solution.py:55
  214.5 15.1 %collective-permute-start.27 = (bf16[128,768]{1,0:T(8,128)(2,1)S(1)}, bf16[128,768]{1,0:T(8,128)(2,1)S(1)}, u32[]{:S(2)}, u32[]{:S(2)}) collective-permute-start(bf16[128,768]{1,0:T(8,128)(2,1)S(1)} %get-tuple-element.446), channel_id=1, source_target_pairs={{0,16},{1,17},{4,20},{5,21},{8,24},{9,25},{12,28},{13,29},{16,18},... | collective-permute-start | bytes 589832 | tf_op jit(solution)/shard_map/ppermute | solution.py:55
  228.2 15.1 %collective-permute-start.30 = (bf16[128,768]{1,0:T(8,128)(2,1)S(1)}, bf16[128,768]{1,0:T(8,128)(2,1)S(1)}, u32[]{:S(2)}, u32[]{:S(2)}) collective-permute-start(bf16[128,768]{1,0:T(8,128)(2,1)S(1)} %get-tuple-element.489), channel_id=1, source_target_pairs={{0,16},{1,17},{4,20},{5,21},{8,24},{9,25},{12,28},{13,29},{16,18},... | collective-permute-start | bytes 589832 | tf_op jit(solution)/shard_map/ppermute | solution.py:55
  250.1 16.5 %collective-permute-start.32 = (bf16[128,768]{1,0:T(8,128)(2,1)S(1)}, bf16[128,768]{1,0:T(8,128)(2,1)S(1)}, u32[]{:S(2)}, u32[]{:S(2)}) collective-permute-start(bf16[128,768]{1,0:T(8,128)(2,1)S(1)} %get-tuple-element.531), channel_id=1, source_target_pairs={{0,16},{1,17},{4,20},{5,21},{8,24},{9,25},{12,28},{13,29},{16,18},... | collective-permute-start | bytes 589832 | tf_op jit(solution)/shard_map/ppermute | solution.py:55
  252.3 17.5 %collective-permute-start.31 = (bf16[128,768]{1,0:T(8,128)(2,1)S(1)}, bf16[128,768]{1,0:T(8,128)(2,1)S(1)}, u32[]{:S(2)}, u32[]{:S(2)}) collective-permute-start(bf16[128,768]{1,0:T(8,128)(2,1)S(1)} %get-tuple-element.530), channel_id=1, source_target_pairs={{0,16},{1,17},{4,20},{5,21},{8,24},{9,25},{12,28},{13,29},{16,18},... | collective-permute-start | bytes 589832 | tf_op jit(solution)/shard_map/ppermute | solution.py:55
  266.9 14.8 %collective-permute-start.34 = (bf16[128,768]{1,0:T(8,128)(2,1)S(1)}, bf16[128,768]{1,0:T(8,128)(2,1)S(1)}, u32[]{:S(2)}, u32[]{:S(2)}) collective-permute-start(bf16[128,768]{1,0:T(8,128)(2,1)S(1)} %get-tuple-element.573), channel_id=1, source_target_pairs={{0,16},{1,17},{4,20},{5,21},{8,24},{9,25},{12,28},{13,29},{16,18},... | collective-permute-start | bytes 589832 | tf_op jit(solution)/shard_map/ppermute | solution.py:55
  292.3 12.1 %collective-permute-start.36 = (bf16[128,768]{1,0:T(8,128)(2,1)S(1)}, bf16[128,768]{1,0:T(8,128)(2,1)S(1)}, u32[]{:S(2)}, u32[]{:S(2)}) collective-permute-start(bf16[128,768]{1,0:T(8,128)(2,1)S(1)} %get-tuple-element.636), channel_id=1, source_target_pairs={{2,18},{3,19},{6,22},{7,23},{10,26},{11,27},{14,30},{15,31},{16,0}... | collective-permute-start | bytes 589832 | tf_op jit(solution)/shard_map/ppermute | solution.py:55
  293.9 14.7 %collective-permute-start.35 = (bf16[128,768]{1,0:T(8,128)(2,1)S(1)}, bf16[128,768]{1,0:T(8,128)(2,1)S(1)}, u32[]{:S(2)}, u32[]{:S(2)}) collective-permute-start(bf16[128,768]{1,0:T(8,128)(2,1)S(1)} %get-tuple-element.635), channel_id=1, source_target_pairs={{2,18},{3,19},{6,22},{7,23},{10,26},{11,27},{14,30},{15,31},{16,0}... | collective-permute-start | bytes 589832 | tf_op jit(solution)/shard_map/ppermute | solution.py:55
  304.6 22.3 %collective-permute-start.38 = (bf16[128,768]{1,0:T(8,128)(2,1)S(1)}, bf16[128,768]{1,0:T(8,128)(2,1)S(1)}, u32[]{:S(2)}, u32[]{:S(2)}) collective-permute-start(bf16[128,768]{1,0:T(8,128)(2,1)S(1)} %get-tuple-element.656), channel_id=1, source_target_pairs={{2,18},{3,19},{6,22},{7,23},{10,26},{11,27},{14,30},{15,31},{16,0}... | collective-permute-start | bytes 589832 | tf_op jit(solution)/shard_map/ppermute | solution.py:55
  315.5 19.9 %collective-permute-start.37 = (bf16[128,768]{1,0:T(8,128)(2,1)S(1)}, bf16[128,768]{1,0:T(8,128)(2,1)S(1)}, u32[]{:S(2)}, u32[]{:S(2)}) collective-permute-start(bf16[128,768]{1,0:T(8,128)(2,1)S(1)} %get-tuple-element.655), channel_id=1, source_target_pairs={{2,18},{3,19},{6,22},{7,23},{10,26},{11,27},{14,30},{15,31},{16,0}... | collective-permute-start | bytes 589832 | tf_op jit(solution)/shard_map/ppermute | solution.py:55
  327.1 49.5 %collective-permute-start.40 = (bf16[128,768]{1,0:T(8,128)(2,1)S(1)}, bf16[128,768]{1,0:T(8,128)(2,1)S(1)}, u32[]{:S(2)}, u32[]{:S(2)}) collective-permute-start(bf16[128,768]{1,0:T(8,128)(2,1)S(1)} %get-tuple-element.676), channel_id=1, source_target_pairs={{2,18},{3,19},{6,22},{7,23},{10,26},{11,27},{14,30},{15,31},{16,0}... | collective-permute-start | bytes 589832 | tf_op jit(solution)/shard_map/ppermute | solution.py:55
  335.6 59.3 %collective-permute-start.39 = (bf16[128,768]{1,0:T(8,128)(2,1)S(1)}, bf16[128,768]{1,0:T(8,128)(2,1)S(1)}, u32[]{:S(2)}, u32[]{:S(2)}) collective-permute-start(bf16[128,768]{1,0:T(8,128)(2,1)S(1)} %get-tuple-element.675), channel_id=1, source_target_pairs={{2,18},{3,19},{6,22},{7,23},{10,26},{11,27},{14,30},{15,31},{16,0}... | collective-permute-start | bytes 589832 | tf_op jit(solution)/shard_map/ppermute | solution.py:55
  393.2 20.3 %collective-permute-start.42 = (bf16[128,768]{1,0:T(8,128)(2,1)S(1)}, bf16[128,768]{1,0:T(8,128)(2,1)S(1)}, u32[]{:S(2)}, u32[]{:S(2)}) collective-permute-start(bf16[128,768]{1,0:T(8,128)(2,1)S(1)} %get-tuple-element.696), channel_id=1, source_target_pairs={{2,18},{3,19},{6,22},{7,23},{10,26},{11,27},{14,30},{15,31},{16,0}... | collective-permute-start | bytes 589832 | tf_op jit(solution)/shard_map/ppermute | solution.py:55
  410.7 20.6 %collective-permute-start.41 = (bf16[128,768]{1,0:T(8,128)(2,1)S(1)}, bf16[128,768]{1,0:T(8,128)(2,1)S(1)}, u32[]{:S(2)}, u32[]{:S(2)}) collective-permute-start(bf16[128,768]{1,0:T(8,128)(2,1)S(1)} %get-tuple-element.695), channel_id=1, source_target_pairs={{2,18},{3,19},{6,22},{7,23},{10,26},{11,27},{14,30},{15,31},{16,0}... | collective-permute-start | bytes 589832 | tf_op jit(solution)/shard_map/ppermute | solution.py:55
  449.6 24.9 %collective-permute-start.43 = (bf16[4,32,768]{2,1,0:T(8,128)(2,1)S(1)}, bf16[4,32,768]{2,1,0:T(8,128)(2,1)S(1)}, u32[]{:S(2)}, u32[]{:S(2)}) collective-permute-start(bf16[4,32,768]{2,1,0:T(8,128)(2,1)S(1)} %get-tuple-element.836), channel_id=1, source_target_pairs={{0,1},{1,17},{2,3},{3,19},{4,5},{5,21},{6,7},{7,23},{8,9},{9,25},{... | collective-permute-start | bytes 589832 | tf_op jit(solution)/shard_map/ppermute | solution.py:55
  451.2 23.9 %collective-permute-start.44 = (bf16[4,32,768]{2,1,0:T(8,128)(2,1)S(1)}, bf16[4,32,768]{2,1,0:T(8,128)(2,1)S(1)}, u32[]{:S(2)}, u32[]{:S(2)}) collective-permute-start(bf16[4,32,768]{2,1,0:T(8,128)(2,1)S(1)} %get-tuple-element.835), channel_id=1, source_target_pairs={{0,0},{1,16},{2,2},{3,18},{4,4},{5,20},{6,6},{7,22},{8,8},{9,24},{... | collective-permute-start | bytes 589832 | tf_op jit(solution)/shard_map/ppermute | solution.py:55
  451.9 23.2 %collective-permute-start.45 = (bf16[4,32,768]{2,1,0:T(8,128)(2,1)S(1)}, bf16[4,32,768]{2,1,0:T(8,128)(2,1)S(1)}, u32[]{:S(2)}, u32[]{:S(2)}) collective-permute-start(bf16[4,32,768]{2,1,0:T(8,128)(2,1)S(1)} %get-tuple-element.834), channel_id=1, source_target_pairs={{0,3},{1,19},{2,1},{3,17},{4,7},{5,23},{6,5},{7,21},{8,11},{9,27},... | collective-permute-start | bytes 589832 | tf_op jit(solution)/shard_map/ppermute | solution.py:55
  453.2 21.9 %collective-permute-start.46 = (bf16[4,32,768]{2,1,0:T(8,128)(2,1)S(1)}, bf16[4,32,768]{2,1,0:T(8,128)(2,1)S(1)}, u32[]{:S(2)}, u32[]{:S(2)}) collective-permute-start(bf16[4,32,768]{2,1,0:T(8,128)(2,1)S(1)} %get-tuple-element.833), channel_id=1, source_target_pairs={{0,2},{1,18},{2,0},{3,16},{4,6},{5,22},{6,4},{7,20},{8,10},{9,26},... | collective-permute-start | bytes 589832 | tf_op jit(solution)/shard_map/ppermute | solution.py:55
  472.4 20.1 %collective-permute-start.51 = (bf16[480,768]{1,0:T(8,128)(2,1)}, bf16[480,768]{1,0:T(8,128)(2,1)S(1)}, u32[]{:S(2)}, u32[]{:S(2)}) collective-permute-start(bf16[480,768]{1,0:T(8,128)(2,1)} %get-tuple-element.730), channel_id=1, source_target_pairs={{0,1},{1,0},{2,3},{3,2},{4,5},{5,4},{6,7},{7,6},{8,9},{9,8},{10,11... | collective-permute-start | bytes 2211848 | tf_op jit(solution)/shard_map/ppermute | solution.py:55
  474.6 18.5 %collective-permute-start.48 = (bf16[480,768]{1,0:T(8,128)(2,1)}, bf16[480,768]{1,0:T(8,128)(2,1)S(1)}, u32[]{:S(2)}, u32[]{:S(2)}) collective-permute-start(bf16[480,768]{1,0:T(8,128)(2,1)} %get-tuple-element.726), channel_id=1, source_target_pairs={{0,1},{1,0},{2,3},{3,2},{4,5},{5,4},{6,7},{7,6},{8,9},{9,8},{10,11... | collective-permute-start | bytes 2211848 | tf_op jit(solution)/shard_map/ppermute | solution.py:55
  494.5 19.4 %collective-permute-start.52 = (bf16[480,768]{1,0:T(8,128)(2,1)S(1)}, bf16[480,768]{1,0:T(8,128)(2,1)S(1)}, u32[]{:S(2)}, u32[]{:S(2)}) collective-permute-start(bf16[480,768]{1,0:T(8,128)(2,1)S(1)} %add_convert_fusion.23), channel_id=1, source_target_pairs={{0,4},{1,5},{2,6},{3,7},{4,0},{5,1},{6,2},{7,3},{8,12},{9,13},{10,... | collective-permute-start | bytes 2211848 | tf_op jit(solution)/shard_map/ppermute | solution.py:55
  496.9 20.0 %collective-permute-start.55 = (bf16[496,768]{1,0:T(8,128)(2,1)S(1)}, bf16[496,768]{1,0:T(8,128)(2,1)S(1)}, u32[]{:S(2)}, u32[]{:S(2)}) collective-permute-start(bf16[496,768]{1,0:T(8,128)(2,1)S(1)} %add_convert_fusion.12), channel_id=1, source_target_pairs={{0,8},{1,9},{2,10},{3,11},{4,12},{5,13},{6,14},{7,15},{8,0},{9,1},... | collective-permute-start | bytes 2285576 | tf_op jit(solution)/shard_map/ppermute | solution.py:55
  498.4 33.7 %collective-permute-start.62 = (bf16[480,768]{1,0:T(8,128)(2,1)S(1)}, bf16[480,768]{1,0:T(8,128)(2,1)S(1)}, u32[]{:S(2)}, u32[]{:S(2)}) collective-permute-start(bf16[480,768]{1,0:T(8,128)(2,1)S(1)} %copy-done.38), channel_id=1, source_target_pairs={{0,1},{1,0},{2,3},{3,2},{4,5},{5,4},{6,7},{7,6},{8,9},{9,8},{10,11... | collective-permute-start | bytes 2211848 | tf_op jit(solution)/shard_map/ppermute | solution.py:55
  498.5 30.7 %collective-permute-start.49 = (bf16[480,768]{1,0:T(8,128)(2,1)S(1)}, bf16[480,768]{1,0:T(8,128)(2,1)S(1)}, u32[]{:S(2)}, u32[]{:S(2)}) collective-permute-start(bf16[480,768]{1,0:T(8,128)(2,1)S(1)} %add_convert_fusion.26), channel_id=1, source_target_pairs={{0,4},{1,5},{2,6},{3,7},{4,0},{5,1},{6,2},{7,3},{8,12},{9,13},{10,... | collective-permute-start | bytes 2211848 | tf_op jit(solution)/shard_map/ppermute | solution.py:55
  500.1 32.0 %collective-permute-start.57 = (bf16[496,768]{1,0:T(8,128)(2,1)S(1)}, bf16[496,768]{1,0:T(8,128)(2,1)S(1)}, u32[]{:S(2)}, u32[]{:S(2)}) collective-permute-start(bf16[496,768]{1,0:T(8,128)(2,1)S(1)} %add_convert_fusion.10), channel_id=1, source_target_pairs={{0,8},{1,9},{2,10},{3,11},{4,12},{5,13},{6,14},{7,15},{8,0},{9,1},... | collective-permute-start | bytes 2285576 | tf_op jit(solution)/shard_map/ppermute | solution.py:55
  513.9 19.9 %collective-permute-start.63 = (bf16[496,768]{1,0:T(8,128)(2,1)S(1)}, bf16[496,768]{1,0:T(8,128)(2,1)S(1)}, u32[]{:S(2)}, u32[]{:S(2)}) collective-permute-start(bf16[496,768]{1,0:T(8,128)(2,1)S(1)} %copy-done.33), channel_id=1, source_target_pairs={{0,1},{1,0},{2,3},{3,2},{4,5},{5,4},{6,7},{7,6},{8,9},{9,8},{10,11... | collective-permute-start | bytes 2285576 | tf_op jit(solution)/shard_map/ppermute | solution.py:55
  516.9 18.8 %collective-permute-start.64 = (bf16[496,768]{1,0:T(8,128)(2,1)S(1)}, bf16[496,768]{1,0:T(8,128)(2,1)S(1)}, u32[]{:S(2)}, u32[]{:S(2)}) collective-permute-start(bf16[496,768]{1,0:T(8,128)(2,1)S(1)} %copy-done.32), channel_id=1, source_target_pairs={{0,1},{1,0},{2,3},{3,2},{4,5},{5,4},{6,7},{7,6},{8,9},{9,8},{10,11... | collective-permute-start | bytes 2285576 | tf_op jit(solution)/shard_map/ppermute | solution.py:55
  532.1 19.3 %collective-permute-start.59 = (bf16[496,768]{1,0:T(8,128)(2,1)S(1)}, bf16[496,768]{1,0:T(8,128)(2,1)S(1)}, u32[]{:S(2)}, u32[]{:S(2)}) collective-permute-start(bf16[496,768]{1,0:T(8,128)(2,1)S(1)} %copy-done.31), channel_id=1, source_target_pairs={{0,1},{1,0},{2,3},{3,2},{4,5},{5,4},{6,7},{7,6},{8,9},{9,8},{10,11... | collective-permute-start | bytes 2285576 | tf_op jit(solution)/shard_map/ppermute | solution.py:55
  532.1 18.9 %collective-permute-start.58 = (bf16[480,768]{1,0:T(8,128)(2,1)S(1)}, bf16[480,768]{1,0:T(8,128)(2,1)S(1)}, u32[]{:S(2)}, u32[]{:S(2)}) collective-permute-start(bf16[480,768]{1,0:T(8,128)(2,1)S(1)} %add_convert_fusion.22), channel_id=1, source_target_pairs={{0,8},{1,9},{2,10},{3,11},{4,12},{5,13},{6,14},{7,15},{8,0},{9,1},... | collective-permute-start | bytes 2211848 | tf_op jit(solution)/shard_map/ppermute | solution.py:55
  533.8 19.1 %collective-permute-start.60 = (bf16[496,768]{1,0:T(8,128)(2,1)S(1)}, bf16[496,768]{1,0:T(8,128)(2,1)S(1)}, u32[]{:S(2)}, u32[]{:S(2)}) collective-permute-start(bf16[496,768]{1,0:T(8,128)(2,1)S(1)} %add_convert_fusion.11), channel_id=1, source_target_pairs={{0,4},{1,5},{2,6},{3,7},{4,0},{5,1},{6,2},{7,3},{8,12},{9,13},{10,... | collective-permute-start | bytes 2285576 | tf_op jit(solution)/shard_map/ppermute | solution.py:55
  535.7 20.2 %collective-permute-start.74 = (bf16[480,768]{1,0:T(8,128)(2,1)S(1)}, bf16[480,768]{1,0:T(8,128)(2,1)S(1)}, u32[]{:S(2)}, u32[]{:S(2)}) collective-permute-start(bf16[480,768]{1,0:T(8,128)(2,1)S(1)} %copy-done.36), channel_id=1, source_target_pairs={{0,1},{1,0},{2,3},{3,2},{4,5},{5,4},{6,7},{7,6},{8,9},{9,8},{10,11... | collective-permute-start | bytes 2211848 | tf_op jit(solution)/shard_map/ppermute | solution.py:55
  553.5 19.5 %collective-permute-start.75 = (bf16[480,768]{1,0:T(8,128)(2,1)S(1)}, bf16[480,768]{1,0:T(8,128)(2,1)S(1)}, u32[]{:S(2)}, u32[]{:S(2)}) collective-permute-start(bf16[480,768]{1,0:T(8,128)(2,1)S(1)} %add_convert_fusion.19), channel_id=1, source_target_pairs={{0,4},{1,5},{2,6},{3,7},{4,0},{5,1},{6,2},{7,3},{8,12},{9,13},{10,... | collective-permute-start | bytes 2211848 | tf_op jit(solution)/shard_map/ppermute | solution.py:55
  555.1 19.7 %collective-permute-start.68 = (bf16[496,768]{1,0:T(8,128)(2,1)S(1)}, bf16[496,768]{1,0:T(8,128)(2,1)S(1)}, u32[]{:S(2)}, u32[]{:S(2)}) collective-permute-start(bf16[496,768]{1,0:T(8,128)(2,1)S(1)} %copy-done.30), channel_id=1, source_target_pairs={{0,1},{1,0},{2,3},{3,2},{4,5},{5,4},{6,7},{7,6},{8,9},{9,8},{10,11... | collective-permute-start | bytes 2285576 | tf_op jit(solution)/shard_map/ppermute | solution.py:55
  555.1 34.2 %collective-permute-start.69 = (bf16[496,768]{1,0:T(8,128)(2,1)S(1)}, bf16[496,768]{1,0:T(8,128)(2,1)S(1)}, u32[]{:S(2)}, u32[]{:S(2)}) collective-permute-start(bf16[496,768]{1,0:T(8,128)(2,1)S(1)} %add_convert_fusion.5), channel_id=1, source_target_pairs={{0,4},{1,5},{2,6},{3,7},{4,0},{5,1},{6,2},{7,3},{8,12},{9,13},{10,... | collective-permute-start | bytes 2285576 | tf_op jit(solution)/shard_map/ppermute | solution.py:55
  555.7 33.9 %collective-permute-start.72 = (bf16[480,768]{1,0:T(8,128)(2,1)S(1)}, bf16[480,768]{1,0:T(8,128)(2,1)S(1)}, u32[]{:S(2)}, u32[]{:S(2)}) collective-permute-start(bf16[480,768]{1,0:T(8,128)(2,1)S(1)} %copy-done.35), channel_id=1, source_target_pairs={{0,1},{1,0},{2,3},{3,2},{4,5},{5,4},{6,7},{7,6},{8,9},{9,8},{10,11... | collective-permute-start | bytes 2211848 | tf_op jit(solution)/shard_map/ppermute | solution.py:55
  555.9 35.5 %collective-permute-start.77 = (bf16[480,768]{1,0:T(8,128)(2,1)S(1)}, bf16[480,768]{1,0:T(8,128)(2,1)S(1)}, u32[]{:S(2)}, u32[]{:S(2)}) collective-permute-start(bf16[480,768]{1,0:T(8,128)(2,1)S(1)} %add_convert_fusion.21), channel_id=1, source_target_pairs={{0,16},{1,17},{2,18},{3,19},{4,20},{5,21},{6,22},{7,23},{8,24},{9,... | collective-permute-start | bytes 2211848 | tf_op jit(solution)/shard_map/ppermute | solution.py:55
  572.9 32.1 %collective-permute-start.73 = (bf16[480,768]{1,0:T(8,128)(2,1)S(1)}, bf16[480,768]{1,0:T(8,128)(2,1)S(1)}, u32[]{:S(2)}, u32[]{:S(2)}) collective-permute-start(bf16[480,768]{1,0:T(8,128)(2,1)S(1)} %add_convert_fusion.20), channel_id=1, source_target_pairs={{0,4},{1,5},{2,6},{3,7},{4,0},{5,1},{6,2},{7,3},{8,12},{9,13},{10,... | collective-permute-start | bytes 2211848 | tf_op jit(solution)/shard_map/ppermute | solution.py:55
  574.8 31.4 %collective-permute-start.76 = (bf16[480,768]{1,0:T(8,128)(2,1)S(1)}, bf16[480,768]{1,0:T(8,128)(2,1)S(1)}, u32[]{:S(2)}, u32[]{:S(2)}) collective-permute-start(bf16[480,768]{1,0:T(8,128)(2,1)S(1)} %add_convert_fusion.15), channel_id=1, source_target_pairs={{0,8},{1,9},{2,10},{3,11},{4,12},{5,13},{6,14},{7,15},{8,0},{9,1},... | collective-permute-start | bytes 2211848 | tf_op jit(solution)/shard_map/ppermute | solution.py:55
  589.3 18.6 %collective-permute-start.66 = (bf16[496,768]{1,0:T(8,128)(2,1)S(1)}, bf16[496,768]{1,0:T(8,128)(2,1)S(1)}, u32[]{:S(2)}, u32[]{:S(2)}) collective-permute-start(bf16[496,768]{1,0:T(8,128)(2,1)S(1)} %copy-done.29), channel_id=1, source_target_pairs={{0,1},{1,0},{2,3},{3,2},{4,5},{5,4},{6,7},{7,6},{8,9},{9,8},{10,11... | collective-permute-start | bytes 2285576 | tf_op jit(solution)/shard_map/ppermute | solution.py:55
  589.6 36.8 %collective-permute-start.65 = (bf16[496,768]{1,0:T(8,128)(2,1)S(1)}, bf16[496,768]{1,0:T(8,128)(2,1)S(1)}, u32[]{:S(2)}, u32[]{:S(2)}) collective-permute-start(bf16[496,768]{1,0:T(8,128)(2,1)S(1)} %add_convert_fusion.7), channel_id=1, source_target_pairs={{0,16},{1,17},{2,18},{3,19},{4,20},{5,21},{6,22},{7,23},{8,24},{9,... | collective-permute-start | bytes 2285576 | tf_op jit(solution)/shard_map/ppermute | solution.py:55
  591.4 35.1 %collective-permute-start.67 = (bf16[496,768]{1,0:T(8,128)(2,1)S(1)}, bf16[496,768]{1,0:T(8,128)(2,1)S(1)}, u32[]{:S(2)}, u32[]{:S(2)}) collective-permute-start(bf16[496,768]{1,0:T(8,128)(2,1)S(1)} %add_convert_fusion.6), channel_id=1, source_target_pairs={{0,4},{1,5},{2,6},{3,7},{4,0},{5,1},{6,2},{7,3},{8,12},{9,13},{10,... | collective-permute-start | bytes 2285576 | tf_op jit(solution)/shard_map/ppermute | solution.py:55
  605.1 32.4 %collective-permute-start.70 = (bf16[496,768]{1,0:T(8,128)(2,1)S(1)}, bf16[496,768]{1,0:T(8,128)(2,1)S(1)}, u32[]{:S(2)}, u32[]{:S(2)}) collective-permute-start(bf16[496,768]{1,0:T(8,128)(2,1)S(1)} %add_convert_fusion.1), channel_id=1, source_target_pairs={{0,8},{1,9},{2,10},{3,11},{4,12},{5,13},{6,14},{7,15},{8,0},{9,1},... | collective-permute-start | bytes 2285576 | tf_op jit(solution)/shard_map/ppermute | solution.py:55
  607.7 33.7 %collective-permute-start.78 = (bf16[480,768]{1,0:T(8,128)(2,1)}, bf16[480,768]{1,0:T(8,128)(2,1)}, u32[]{:S(2)}, u32[]{:S(2)}) collective-permute-start(bf16[480,768]{1,0:T(8,128)(2,1)} %get-tuple-element.827), channel_id=1, source_target_pairs={{0,1},{1,0},{2,3},{3,2},{4,5},{5,4},{6,7},{7,6},{8,9},{9,8},{10,11... | collective-permute-start | bytes 2211848 | tf_op jit(solution)/shard_map/ppermute | solution.py:55
  (56 other events, 658.1 us)
